TPU v7x, 128 devices: a whole 4x4x4 slice. The times are simulated.
128 devices in a mesh: sub: 32 (over y, x, core), gy: 4 (over z).
Axes of the slice: x: 4, y: 4, z: 4, core: 2. Of those that a mesh axis runs over, the one named last changes fastest.
Arguments:
- a_vals: bfloat16 [64, 64, 64, 320], P('sub', 'gy'), may hold values from -0.75 to 0.75
- p_vals: bfloat16 [64, 64, 64, 128], P('sub', 'gy'), may hold values from -0.75 to 0.75
- spill_axis: int32 [64, 64], P('sub', 'gy'), may hold values from 0 to 1
Outputs:
- coarse: bfloat16 [32, 32, 64, 1600], P('sub', 'gy')
Inputs may be any that keep to these rules, and one draw needn't show every extreme that they name: `spill_axis`: 0 puts the second aggregate across the nearer aggregate face along the slab, 1 across it.
All inputs are finite; a program needn't handle non-finite values.
Results may differ from a plain program's by a relative error of at most 0.007.
Values may be sent and summed in bfloat16 or wider, within the bound.
A program may use at most 384 MiB of HBM per device.

v0:
```python
import jax
import jax.numpy as jnp
from jax import lax
from jax.sharding import PartitionSpec as P

SLOTS = 25


OFFSETS = ((0, 0), (-1, 0), (1, 0), (0, -1), (0, 1))


def with_halo(block, sides, width):
    for axis, dim in sides:
        count = lax.axis_size(axis)
        forward = [(i, i + 1) for i in range(count - 1)]
        backward = [(target, source) for source, target in forward]
        low = lax.ppermute(
            lax.slice_in_dim(block, block.shape[dim] - width, None, axis=dim), axis, forward
        )
        high = lax.ppermute(lax.slice_in_dim(block, 0, width, axis=dim), axis, backward)
        block = jnp.concatenate([low, block, high], axis=dim)
    return block


def passed_along(value, axis, steps):
    count = lax.axis_size(axis)
    leading, last = (max(0, -steps), min(count, count - steps))
    return lax.ppermute(value, axis, [(source, source + steps) for source in range(leading, last)])


def candidates(which, odd_x, odd_y, spill):
    if which == 0:
        return [(0, 0, None)]
    return [(2 * odd_x - 1, 0, spill == 0), (0, 2 * odd_y - 1, spill == 1)]


def assemble(a_reg, p_ext, sp_ext, base_x, base_y, total_x, total_y):
    rows_f = a_reg.shape[0]
    cols_f = a_reg.shape[1]
    width = p_ext.shape[2]
    half_r = rows_f // 2
    half_c = cols_f // 2
    xs = base_x + jnp.arange(rows_f, dtype=jnp.int32)[:, None] + jnp.zeros((1, cols_f), jnp.int32)
    ys = base_y + jnp.zeros((rows_f, 1), jnp.int32) + jnp.arange(cols_f, dtype=jnp.int32)[None, :]
    own_p = p_ext[1 : rows_f + 1, 1 : cols_f + 1]
    own_sp = sp_ext[1 : rows_f + 1, 1 : cols_f + 1]
    left = own_p.reshape(rows_f, cols_f, width, 2, width)
    dense = jnp.zeros((half_r + 2, half_c + 2, SLOTS, width, width), jnp.float32)
    for k in range(5):
        shift_s, shift_g = OFFSETS[k]
        near_p = p_ext[1 + shift_s : 1 + shift_s + rows_f, 1 + shift_g : 1 + shift_g + cols_f]
        near_sp = sp_ext[1 + shift_s : 1 + shift_s + rows_f, 1 + shift_g : 1 + shift_g + cols_f]
        block_a = a_reg[:, :, :, k * width : (k + 1) * width]
        product = jnp.einsum(
            "xyab,xybc->xyac", block_a, near_p, preferred_element_type=jnp.float32
        ).astype(jnp.bfloat16)
        right = product.reshape(rows_f, cols_f, width, 2, width)
        for which_p in range(2):
            for which_q in range(2):
                term = jnp.einsum(
                    "xyba,xybc->xyac",
                    left[:, :, :, which_p],
                    right[:, :, :, which_q],
                    preferred_element_type=jnp.float32,
                )
                term = term.reshape(half_r, 2, half_c, 2, width, width)
                for odd_x in range(2):
                    for odd_y in range(2):
                        piece = term[:, odd_x, :, odd_y]
                        half_x = xs[odd_x::2, odd_y::2] // 2
                        half_y = ys[odd_x::2, odd_y::2] // 2
                        own_s = own_sp[odd_x::2, odd_y::2]
                        near_s = near_sp[odd_x::2, odd_y::2]
                        near_x = odd_x + shift_s
                        near_y = odd_y + shift_g
                        start_s = near_x // 2
                        start_g = near_y // 2
                        row_list = candidates(which_p, odd_x, odd_y, own_s)
                        col_list = [
                            (start_s + cs, start_g + cg, cmask)
                            for cs, cg, cmask in candidates(which_q, near_x % 2, near_y % 2, near_s)
                        ]
                        for row_s, row_g, row_mask in row_list:
                            for col_s, col_g, col_mask in col_list:
                                agg_x = half_x + row_s
                                agg_y = half_y + row_g
                                col_x = half_x + col_s
                                col_y = half_y + col_g
                                valid = (
                                    (agg_x >= 0)
                                    & (agg_x < total_x)
                                    & (agg_y >= 0)
                                    & (agg_y < total_y)
                                )
                                valid = (
                                    valid
                                    & (col_x >= 0)
                                    & (col_x < total_x)
                                    & (col_y >= 0)
                                    & (col_y < total_y)
                                )
                                if row_mask is not None:
                                    valid = valid & row_mask
                                if col_mask is not None:
                                    valid = valid & col_mask
                                slot = (col_s - row_s + 2) * 5 + (col_g - row_g + 2)
                                masked = jnp.where(valid[:, :, None, None], piece, 0.0)
                                dense = dense.at[
                                    1 + row_s : 1 + row_s + half_r,
                                    1 + row_g : 1 + row_g + half_c,
                                    slot,
                                ].add(masked)
    return dense


def local(a_vals, p_vals, spill_axis):
    rows_f = a_vals.shape[0]
    cols_f = a_vals.shape[1]
    width = p_vals.shape[2]
    total_x = rows_f * lax.axis_size("sub") // 2
    total_y = cols_f * lax.axis_size("gy") // 2
    anchor_x = lax.axis_index("sub") * rows_f
    anchor_y = lax.axis_index("gy") * cols_f
    p_ext, sp_ext = (
        with_halo(p_vals, (("sub", 0), ("gy", 1)), 1),
        with_halo(spill_axis, (("sub", 0), ("gy", 1)), 1),
    )
    whole = assemble(a_vals, p_ext, sp_ext, anchor_x, anchor_y, total_x, total_y)
    owned = whole[1:-1, 1:-1]
    from_next = passed_along(whole[0, 1:-1].astype(jnp.bfloat16), "sub", -1).astype(jnp.float32)
    from_prev = passed_along(whole[-1, 1:-1].astype(jnp.bfloat16), "sub", 1).astype(jnp.float32)
    owned = owned.at[-1].add(from_next)
    owned = owned.at[0].add(from_prev)
    side_next = passed_along(whole[1:-1, 0].astype(jnp.bfloat16), "gy", -1).astype(jnp.float32)
    side_prev = passed_along(whole[1:-1, -1].astype(jnp.bfloat16), "gy", 1).astype(jnp.float32)
    owned = owned.at[:, -1].add(side_next)
    owned = owned.at[:, 0].add(side_prev)
    shaped = owned.transpose(0, 1, 3, 2, 4).reshape(rows_f // 2, cols_f // 2, width, SLOTS * width)
    return shaped.astype(jnp.bfloat16)


def solution(mesh):
    return jax.shard_map(
        local,
        mesh=mesh,
        in_specs=(P("sub", "gy", None, None), P("sub", "gy", None, None), P("sub", "gy")),
        out_specs=P("sub", "gy", None, None),
        check_vma=False,
    )
```

profile of v0, /device:TPU:40, one launch (start us, length us, event | category | flops | bytes accessed | tf_op | source)
XLA Modules:
  0.0 658.0 jit_solution(7079850700185191779)
XLA Ops:
  2.7 5.8 collective-permute-start.3
  12.3 5.8 collective-permute-start.2
  27.3 2.4 reshape.10919
  29.7 3.1 fusion.336
  34.7 3.3 fusion.338
  38.0 2.4 copy.283
  40.4 2.4 copy.289
  64.5 3.8 collective-permute-start.5
  68.4 2.5 collective-permute-start.7
  70.9 3.0 collective-permute-done.7
  78.6 11.3 %scatter-add.606 = f32[3,10,25,64,64]{4,3,2,1,0:T(8,128)} pad(f32[1,8,1,64,64]{4,3,2,1,0:T(8,128)S(1)} %bitcast_select_fusion.179, f32[]{:T(128)} %constant.4745.clone.1), padding=1_1x1_1x12_12x0_0x0_0 | pad | bytes 12419076 | tf_op jit(solution)/shard_map/scatter-add | solution.py:112
  152.2 17.6 %copy.412 = f32[3,10,25,64,64]{4,3,2,1,0:T(8,128)} copy(f32[3,10,25,64,64]{4,3,2,1,0:T(8,128)} %fusion.190) | data formatting | bytes 24576000
  172.3 3.2 fusion.332
  175.5 2.4 copy.303
  180.4 2.4 copy.308
  187.1 3.3 fusion.327
  190.4 2.5 copy.321
  195.4 2.4 copy.326
  288.8 17.7 %copy.448 = f32[3,10,25,64,64]{4,3,2,1,0:T(8,128)} copy(f32[3,10,25,64,64]{4,3,2,1,0:T(8,128)} %fusion.159) | data formatting | bytes 24576000
  360.8 3.5 collective-permute-start.4
  403.8 3.1 fusion.322
  406.9 2.4 copy.339
  416.9 3.1 fusion.316
  582.0 9.7 %convert.18 = bf16[3,10,25,64,64]{4,3,2,1,0:T(8,128)(2,1)S(1)} convert(f32[3,10,25,64,64]{4,3,2,1,0:T(8,128)} %fusion.56) | non-fusion elementwise | flops 3072000 | bytes 18432000 | tf_op jit(solution)/shard_map/convert.7
  591.7 3.3 slice_bitcast_fusion.1
  596.9 2.4 collective-permute-start.9
  601.3 4.2 collective-permute-start.11
  605.5 27.9 %collective-permute-done.8 = bf16[8,25,64,64]{3,2,1,0:T(8,128)(2,1)S(1)} collective-permute-done((bf16[8,25,64,64]{3,2,1,0:T(8,128)(2,1)}, bf16[8,25,64,64]{3,2,1,0:T(8,128)(2,1)S(1)}, u32[]{:S(2)}, u32[]{:S(2)}) %collective-permute-start.8) | collective-permute-done | bytes 1638432 | tf_op jit(solution)/shard_map/ppermute | solution.py:28
  633.4 5.6 collective-permute-done.9
  639.0 4.8 fusion
  647.1 4.4 copy.282
  651.5 6.3 convert_element_type.95
  (509 shorter events, 473.5 us)
Async XLA Ops:
  0.8 60.8 %collective-permute-start.1 = (s32[1,16]{1,0:T(1,128)S(1)}, s32[1,16]{1,0:T(1,128)S(1)}, u32[]{:S(2)}, u32[]{:S(2)}) collective-permute-start(s32[1,16]{1,0:T(1,128)S(1)} %get-tuple-element.2558), channel_id=1, source_target_pairs={{0,4},{4,8},{8,12},{12,16},{16,20},{20,24},{24,28},{28,32},{32,36}... | collective-permute-start | bytes 200 | tf_op jit(solution)/shard_map/ppermute | solution.py:17
  2.7 58.8 %collective-permute-start.3 = (s32[1,16]{1,0:T(1,128)S(1)}, s32[1,16]{1,0:T(1,128)S(1)}, u32[]{:S(2)}, u32[]{:S(2)}) collective-permute-start(s32[1,16]{1,0:T(1,128)S(1)} %get-tuple-element.2559), channel_id=1, source_target_pairs={{4,0},{8,4},{12,8},{16,12},{20,16},{24,20},{28,24},{32,28},{36,32}... | collective-permute-start | bytes 200 | tf_op jit(solution)/shard_map/ppermute | solution.py:20
  10.3 160.1 %collective-permute-start = (bf16[1,16,64,128]{3,2,1,0:T(8,128)(2,1)}, bf16[1,16,64,128]{3,2,1,0:T(8,128)(2,1)}, u32[]{:S(2)}, u32[]{:S(2)}) collective-permute-start(bf16[1,16,64,128]{3,2,1,0:T(8,128)(2,1)} %get-tuple-element.2434), channel_id=1, source_target_pairs={{0,4},{4,8},{8,12},{12,16},{16,20},{20,24},{24,28},{28,32},{32,36}... | collective-permute-start | bytes 786440 | tf_op jit(solution)/shard_map/ppermute | solution.py:17
  12.3 173.1 %collective-permute-start.2 = (bf16[1,16,64,128]{3,2,1,0:T(8,128)(2,1)}, bf16[1,16,64,128]{3,2,1,0:T(8,128)(2,1)}, u32[]{:S(2)}, u32[]{:S(2)}) collective-permute-start(bf16[1,16,64,128]{3,2,1,0:T(8,128)(2,1)} %get-tuple-element.2433), channel_id=1, source_target_pairs={{4,0},{8,4},{12,8},{16,12},{20,16},{24,20},{28,24},{32,28},{36,32}... | collective-permute-start | bytes 786440 | tf_op jit(solution)/shard_map/ppermute | solution.py:20
  64.5 6.3 collective-permute-start.5
  68.4 5.5 collective-permute-start.7
  306.5 88.4 %copy-start.52 = (pred[8]{0:T(512)(128)(4,1)S(1)}, pred[8]{0:T(512)(128)(4,1)}, u32[]{:S(2)}) copy-start(pred[8]{0:T(512)(128)(4,1)} %get-tuple-element.2638) | copy-start | bytes 28
  306.5 90.2 %copy-start.51 = (pred[8]{0:T(512)(128)(4,1)S(1)}, pred[8]{0:T(512)(128)(4,1)}, u32[]{:S(2)}) copy-start(pred[8]{0:T(512)(128)(4,1)} %get-tuple-element.2639) | copy-start | bytes 28
  306.5 92.0 %copy-start.50 = (pred[8]{0:T(512)(128)(4,1)S(1)}, pred[8]{0:T(512)(128)(4,1)}, u32[]{:S(2)}) copy-start(pred[8]{0:T(512)(128)(4,1)} %get-tuple-element.2637) | copy-start | bytes 28
  306.5 93.7 %copy-start.49 = (pred[8]{0:T(512)(128)(4,1)S(1)}, pred[8]{0:T(512)(128)(4,1)}, u32[]{:S(2)}) copy-start(pred[8]{0:T(512)(128)(4,1)} %get-tuple-element.2640) | copy-start | bytes 28
  360.8 41.2 %collective-permute-start.4 = (bf16[4,1,64,128]{3,2,1,0:T(8,128)(2,1)S(1)}, bf16[4,1,64,128]{3,2,1,0:T(8,128)(2,1)S(1)}, u32[]{:S(2)}, u32[]{:S(2)}) collective-permute-start(bf16[4,1,64,128]{3,2,1,0:T(8,128)(2,1)S(1)} %get-tuple-element.2358), channel_id=1, source_target_pairs={{0,1},{1,2},{2,3},{4,5},{5,6},{6,7},{8,9},{9,10},{10,11},{12,13},{... | collective-permute-start | bytes 196616 | tf_op jit(solution)/shard_map/ppermute | solution.py:17
  364.3 50.7 %collective-permute-start.6 = (bf16[4,1,64,128]{3,2,1,0:T(8,128)(2,1)S(1)}, bf16[4,1,64,128]{3,2,1,0:T(8,128)(2,1)S(1)}, u32[]{:S(2)}, u32[]{:S(2)}) collective-permute-start(bf16[4,1,64,128]{3,2,1,0:T(8,128)(2,1)S(1)} %get-tuple-element.2357), channel_id=1, source_target_pairs={{1,0},{2,1},{3,2},{5,4},{6,5},{7,6},{9,8},{10,9},{11,10},{13,12},{... | collective-permute-start | bytes 196616 | tf_op jit(solution)/shard_map/ppermute | solution.py:20
  438.1 87.9 %copy-start.41 = (pred[8]{0:T(512)(128)(4,1)S(1)}, pred[8]{0:T(512)(128)(4,1)}, u32[]{:S(2)}) copy-start(pred[8]{0:T(512)(128)(4,1)} %get-tuple-element.2569) | copy-start | bytes 28
  439.9 87.9 %copy-start.40 = (pred[8]{0:T(512)(128)(4,1)S(1)}, pred[8]{0:T(512)(128)(4,1)}, u32[]{:S(2)}) copy-start(pred[8]{0:T(512)(128)(4,1)} %get-tuple-element.2571) | copy-start | bytes 28
  441.8 87.8 %copy-start.43 = (pred[8]{0:T(512)(128)(4,1)S(1)}, pred[8]{0:T(512)(128)(4,1)}, u32[]{:S(2)}) copy-start(pred[8]{0:T(512)(128)(4,1)} %get-tuple-element.2548) | copy-start | bytes 28
  443.6 87.7 %copy-start.42 = (pred[8]{0:T(512)(128)(4,1)S(1)}, pred[8]{0:T(512)(128)(4,1)}, u32[]{:S(2)}) copy-start(pred[8]{0:T(512)(128)(4,1)} %get-tuple-element.2546) | copy-start | bytes 28
  445.5 87.7 %copy-start.39 = (pred[8]{0:T(512)(128)(4,1)S(1)}, pred[8]{0:T(512)(128)(4,1)}, u32[]{:S(2)}) copy-start(pred[8]{0:T(512)(128)(4,1)} %get-tuple-element.2537) | copy-start | bytes 28
  447.3 87.6 %copy-start.38 = (pred[8]{0:T(512)(128)(4,1)S(1)}, pred[8]{0:T(512)(128)(4,1)}, u32[]{:S(2)}) copy-start(pred[8]{0:T(512)(128)(4,1)} %get-tuple-element.2534) | copy-start | bytes 28
  476.7 87.6 %copy-start.28 = (pred[8]{0:T(512)(128)(4,1)S(1)}, pred[8]{0:T(512)(128)(4,1)}, u32[]{:S(2)}) copy-start(pred[8]{0:T(512)(128)(4,1)} %get-tuple-element.2582) | copy-start | bytes 28
  478.0 88.1 %copy-start.26 = (pred[8]{0:T(512)(128)(4,1)S(1)}, pred[8]{0:T(512)(128)(4,1)}, u32[]{:S(2)}) copy-start(pred[8]{0:T(512)(128)(4,1)} %get-tuple-element.2576) | copy-start | bytes 28
  478.0 89.9 %copy-start.33 = (pred[8]{0:T(512)(128)(4,1)S(1)}, pred[8]{0:T(512)(128)(4,1)}, u32[]{:S(2)}) copy-start(pred[8]{0:T(512)(128)(4,1)} %get-tuple-element.2502) | copy-start | bytes 28
  479.7 89.9 %copy-start.32 = (pred[8]{0:T(512)(128)(4,1)S(1)}, pred[8]{0:T(512)(128)(4,1)}, u32[]{:S(2)}) copy-start(pred[8]{0:T(512)(128)(4,1)} %get-tuple-element.2500) | copy-start | bytes 28
  480.6 90.8 %copy-start.31 = (pred[8]{0:T(512)(128)(4,1)S(1)}, pred[8]{0:T(512)(128)(4,1)}, u32[]{:S(2)}) copy-start(pred[8]{0:T(512)(128)(4,1)} %get-tuple-element.2227) | copy-start | bytes 28
  481.5 91.7 %copy-start.27 = (pred[8]{0:T(512)(128)(4,1)S(1)}, pred[8]{0:T(512)(128)(4,1)}, u32[]{:S(2)}) copy-start(pred[8]{0:T(512)(128)(4,1)} %get-tuple-element.2224) | copy-start | bytes 28
  482.7 92.2 %copy-start.25 = (pred[8]{0:T(512)(128)(4,1)S(1)}, pred[8]{0:T(512)(128)(4,1)}, u32[]{:S(2)}) copy-start(pred[8]{0:T(512)(128)(4,1)} %get-tuple-element.2466) | copy-start | bytes 28
  482.7 94.0 %copy-start.24 = (pred[8]{0:T(512)(128)(4,1)S(1)}, pred[8]{0:T(512)(128)(4,1)}, u32[]{:S(2)}) copy-start(pred[8]{0:T(512)(128)(4,1)} %get-tuple-element.2463) | copy-start | bytes 28
  483.0 95.5 %copy-start.23 = (pred[8]{0:T(512)(128)(4,1)S(1)}, pred[8]{0:T(512)(128)(4,1)}, u32[]{:S(2)}) copy-start(pred[8]{0:T(512)(128)(4,1)} %get-tuple-element.2217) | copy-start | bytes 28
  483.2 97.1 %copy-start.22 = (pred[8]{0:T(512)(128)(4,1)S(1)}, pred[8]{0:T(512)(128)(4,1)}, u32[]{:S(2)}) copy-start(pred[8]{0:T(512)(128)(4,1)} %get-tuple-element.2213) | copy-start | bytes 28
  595.0 38.4 %collective-permute-start.8 = (bf16[8,25,64,64]{3,2,1,0:T(8,128)(2,1)}, bf16[8,25,64,64]{3,2,1,0:T(8,128)(2,1)S(1)}, u32[]{:S(2)}, u32[]{:S(2)}) collective-permute-start(bf16[8,25,64,64]{3,2,1,0:T(8,128)(2,1)} %get-tuple-element.2337), channel_id=1, source_target_pairs={{4,0},{8,4},{12,8},{16,12},{20,16},{24,20},{28,24},{32,28},{36,32}... | collective-permute-start | bytes 4915208 | tf_op jit(solution)/shard_map/ppermute | solution.py:28
  596.9 42.1 %collective-permute-start.9 = (bf16[8,25,64,64]{3,2,1,0:T(8,128)(2,1)S(1)}, bf16[8,25,64,64]{3,2,1,0:T(8,128)(2,1)S(1)}, u32[]{:S(2)}, u32[]{:S(2)}) collective-permute-start(bf16[8,25,64,64]{3,2,1,0:T(8,128)(2,1)S(1)} %get-tuple-element.2338), channel_id=1, source_target_pairs={{0,4},{4,8},{8,12},{12,16},{16,20},{20,24},{24,28},{28,32},{32,36}... | collective-permute-start | bytes 4915208 | tf_op jit(solution)/shard_map/ppermute | solution.py:28
  599.4 44.4 %collective-permute-start.10 = (bf16[1,25,64,64]{3,2,1,0:T(8,128)(2,1)S(1)}, bf16[1,25,64,64]{3,2,1,0:T(8,128)(2,1)}, u32[]{:S(2)}, u32[]{:S(2)}) collective-permute-start(bf16[1,25,64,64]{3,2,1,0:T(8,128)(2,1)S(1)} %get-tuple-element.2336), channel_id=1, source_target_pairs={{1,0},{2,1},{3,2},{5,4},{6,5},{7,6},{9,8},{10,9},{11,10},{13,12},{... | collective-permute-start | bytes 614408 | tf_op jit(solution)/shard_map/ppermute | solution.py:28
  601.3 43.7 %collective-permute-start.11 = (bf16[1,25,64,64]{3,2,1,0:T(8,128)(2,1)S(1)}, bf16[1,25,64,64]{3,2,1,0:T(8,128)(2,1)}, u32[]{:S(2)}, u32[]{:S(2)}) collective-permute-start(bf16[1,25,64,64]{3,2,1,0:T(8,128)(2,1)S(1)} %get-tuple-element.2335), channel_id=1, source_target_pairs={{0,1},{1,2},{2,3},{4,5},{5,6},{6,7},{8,9},{9,10},{10,11},{12,13},{... | collective-permute-start | bytes 614408 | tf_op jit(solution)/shard_map/ppermute | solution.py:28
  (42 other events, 2033.1 us)
where the time goes:
time: 671 us; the launch traced here: 658 us
  other arithmetic  337 us (50%)
  local copies, waits for them, and re-layouts  210 us (31%)
  starting transfers between devices  37.9 us (6%)
  waiting for transfers between devices  36.5 us (5%)
  matrix products  29.6 us (4%)
  between operations  7.02 us (1%)
    scatter-add x179, other arithmetic, assemble(): dense = dense.at[1 + row_s:1 + row_s + half_r, 1 + row_g:1 + row_g + half...  313 us
    unnamed x218, local copies, waits for them, and re-layouts  121 us
    ppermute x4, waiting for transfers between devices, passed_along(): lax.ppermute(value, axis, [(source, source + steps) for source in range(l...  33.5 us
    slice x20, local copies, waits for them, and re-layouts, assemble(): piece = term[:, odd_x, :, odd_y]  26.5 us
    dot_general x20, matrix products, assemble(): jnp.einsum('xyba,xybc->xyac', left[:, :, :, which_p], right[:, :, :, whic...  22.4 us
    ppermute x4, starting transfers between devices, with_halo(): lax.ppermute(lax.slice_in_dim(block, 0, width, axis=dim), axis, backward)  16.3 us
    slice x5, local copies, waits for them, and re-layouts, assemble(): right[:, :, :, which_q]  16 us
  transfers between devices with their start and end apart: 12, of which 3 were waited for; matrix products, arithmetic and copies ran while one was open for 32% of the time, Pallas kernels for 0%

commit v1 on v0

v1 whole, which is shorter than its diff:
```python
import functools

import jax
import jax.numpy as jnp
from jax import lax
from jax.experimental import pallas as pl
from jax.experimental.pallas import tpu as pltpu
from jax.sharding import PartitionSpec as P

MESH = pl.DeviceIdType.MESH
F32 = jnp.float32
BF16 = jnp.bfloat16
B = 64
SLOTS = 25


def lanes_low(rows, dtype):
    lane = lax.broadcasted_iota(jnp.int32, (rows, 128), 1)
    return jnp.where(lane < B, 1.0, 0.0).astype(dtype)


def swap_halves(tile):
    return jnp.concatenate([tile[:, B:], tile[:, :B]], axis=1)


def tall(mask):
    return jnp.concatenate([mask] * 4, axis=0)


def transposed_dot(left, right):
    return lax.dot_general(left, right, (((0,), (0,)), ((), ())), preferred_element_type=F32)


def spread(row, cols):
    wide = jnp.broadcast_to(row, (cols, cols))
    at = lax.broadcasted_iota(jnp.int32, (cols, cols), 0)
    lane = lax.broadcasted_iota(jnp.int32, (cols, cols), 1)
    column = jnp.sum(jnp.where(at == lane, wide, 0.0), axis=1, keepdims=True)
    column = jnp.broadcast_to(column, (cols, 128))
    return jnp.broadcast_to(column[:, None, :], (cols, 16, 128))


def kernel(
    n_sub, n_gy, cols,
    a_hbm, p_hbm, sp_hbm, out,
    a_v, pe, sp_own, sp_h, m0t, m1t, rhs, la, lb, gs, msg, rmsg, acc, gl, gr,
    local_sem, sp_send, sp_recv, ps_send, ps_recv, pg_send, pg_recv,
    ms_send, ms_recv, mg_send, mg_recv,
):
    s = lax.axis_index("sub")
    z = lax.axis_index("gy")
    aggs = cols // 2
    chunks = aggs // 2
    before = lax.rem(s + n_sub - 1, n_sub)
    after = lax.rem(s + 1, n_sub)
    lower = lax.rem(z + n_gy - 1, n_gy)
    upper = lax.rem(z + 1, n_gy)
    around = ((before, z), (after, z), (s, lower), (s, upper))
    slow = lax.rem(s, 2)

    barrier = pltpu.get_barrier_semaphore()
    for device in around:
        pl.semaphore_signal(barrier, inc=1, device_id=device, device_id_type=MESH)
    get_sp = pltpu.make_async_copy(sp_hbm, sp_own, local_sem.at[0])
    get_p = pltpu.make_async_copy(p_hbm, pe.at[1:3, 1 : cols + 1], local_sem.at[1])
    get_a = pltpu.make_async_copy(a_hbm, a_v, local_sem.at[2])
    get_sp.start()
    get_p.start()
    get_a.start()
    pl.semaphore_wait(barrier, 4)

    def remote(src, dst, send, recv, device):
        return pltpu.make_async_remote_copy(
            src_ref=src, dst_ref=dst, send_sem=send, recv_sem=recv, device_id=device, device_id_type=MESH
        )

    sp_copies = [
        remote(sp_hbm, sp_h.at[d ^ 1], sp_send.at[d], sp_recv.at[d ^ 1], around[d]) for d in range(4)
    ]
    pg_copies = [
        remote(p_hbm.at[:, 0], pe.at[1:3, cols + 1], pg_send.at[0], pg_recv.at[1], around[2]),
        remote(p_hbm.at[:, cols - 1], pe.at[1:3, 0], pg_send.at[1], pg_recv.at[0], around[3]),
    ]

    def ps_copy(r, c):
        device = (lax.rem(s + n_sub - 1 + 2 * r, n_sub), z)
        return remote(
            p_hbm.at[r, pl.ds(4 * c, 4)], pe.at[3 * (1 - r), pl.ds(1 + 4 * c, 4)],
            ps_send.at[r, c], ps_recv.at[1 - r, c], device,
        )

    def ps_landing(r, c):
        device = (lax.rem(s + n_sub - 1 + 2 * r, n_sub), z)
        return remote(
            p_hbm.at[r, pl.ds(4 * c, 4)], pe.at[3 * r, pl.ds(1 + 4 * c, 4)],
            ps_send.at[r, c], ps_recv.at[r, c], device,
        )

    def ms_copy(r, c):
        device = (lax.rem(s + n_sub - 1 + 2 * r, n_sub), z)
        return remote(
            msg.at[r, c], rmsg.at[1 - r, c], ms_send.at[r, c], ms_recv.at[1 - r, c], device
        )

    def ms_landing(r, c):
        device = (lax.rem(s + n_sub - 1 + 2 * r, n_sub), z)
        return remote(msg.at[r, c], rmsg.at[r, c], ms_send.at[r, c], ms_recv.at[r, c], device)

    for copy in sp_copies:
        copy.start()
    for copy in pg_copies:
        copy.start()
    for c in range(chunks):
        ps_copy(slow, c).start()
        ps_copy(1 - slow, c).start()

    lo = lanes_low(16, BF16)
    hi = (1.0 - lanes_low(16, F32)).astype(BF16)
    lo32 = lanes_low(B, F32)
    zero = jnp.zeros((B, 128), BF16)

    def flag(condition):
        return jnp.where(condition, 1.0, 0.0).astype(F32)

    has_before, has_after = flag(s > 0), flag(s < n_sub - 1)
    has_lower, has_upper = flag(z > 0), flag(z < n_gy - 1)

    for g in range(aggs):
        for t in (0, 2, 10):
            out[0, g, :, 128 * t : 128 * t + 128] = zero
        out[0, g, :, 1536:] = jnp.zeros((B, B), BF16)
        gs[g, 4, 0] = jnp.zeros((128, 128), BF16)
        gs[g, 3, 1] = jnp.zeros((128, 128), BF16)

    column = lax.broadcasted_iota(jnp.int32, (1, cols), 1)
    side_ok = jnp.where(column == 0, has_lower, jnp.where(column == cols - 1, has_upper, 1.0))

    def masks_of_row(row, e, here, reach):
        m0t[e, 1 : cols + 1] = spread((1.0 - row) * (reach * here), cols).astype(BF16)
        m1t[e, 1 : cols + 1] = spread(row * side_ok * here, cols).astype(BF16)

    get_sp.wait()
    own = sp_own[...].astype(F32)
    masks_of_row(own[0:1], 1, F32(1.0), has_before)
    masks_of_row(own[1:2], 2, F32(1.0), has_after)
    get_p.wait()

    def prepare(t, carry):
        r = lax.div(t, aggs)
        g = lax.rem(t, aggs)
        k_in = 2 - r
        for odd in range(2):
            y = 2 * g + odd
            tile = pe[1 + r, 1 + y]
            turned = swap_halves(tile)
            m0 = m0t[1 + r, 1 + y]
            m1 = m1t[1 + r, 1 + y]
            first = turned * tall(m0 * lo)
            only = turned * tall(m1 * lo)
            plain = turned * tall(hi)
            second = only + plain if odd == 0 else plain
            third = zero if odd == 0 else only
            for where_y, k, parts in (
                (y, 0, (first, second, third, zero)),
                (y + 1 - 2 * odd, 4 - (1 - odd), (first, second, third, zero)),
            ):
                for n, part in enumerate(parts):
                    rhs[r, 1 + where_y, k, :, 128 * n : 128 * n + 128] = part
            for n, part in enumerate((zero, second, third, first)):
                rhs[1 - r, 1 + y, 1 + r, :, 128 * n : 128 * n + 128] = part
            if odd == 0:
                outer = (tile * tall(m0 * hi), tile * tall(m1 * hi), tile * tall(lo), zero)
                out_y, out_k = y - 1, 4
            else:
                outer = (zero, tile * tall(lo + m1 * hi), tile * tall(m0 * hi), zero)
                out_y, out_k = y + 1, 3
            for n, part in enumerate(outer):
                rhs[r, 1 + out_y, out_k, :, 128 * n : 128 * n + 128] = part
            la[r, g, B * odd : B * odd + B] = first[:, :B]
            if odd == 0:
                lb[g, r, 0:B, 0:128] = tile * tall(lo + m1 * hi)
                lb[g, r, 0:B, 128:192] = zero[:, :B]
            else:
                lb[g, r, B : 2 * B, 0:128] = tile * tall(lo)
                lb[g, r, B : 2 * B, 128:192] = only[:, :B]
        return carry

    lax.fori_loop(0, 2 * aggs, prepare, 0)

    for copy in sp_copies:
        copy.wait_recv()
    masks_of_row(sp_h[0, 1:2].astype(F32), 0, has_before, F32(1.0))
    masks_of_row(sp_h[1, 0:1].astype(F32), 3, has_after, F32(1.0))
    for copy in pg_copies:
        copy.wait_recv()
    for r, reach in ((0, has_before), (1, has_after)):
        low = jnp.broadcast_to(sp_h[2, r : r + 1, cols - 1 : cols].astype(F32), (16, 128))
        m0 = ((1.0 - low) * (reach * has_lower)).astype(BF16)
        m1 = (low * has_lower).astype(BF16)
        here = jnp.broadcast_to(has_lower, (16, 128)).astype(BF16)
        tile = pe[1 + r, 0]
        for n, part in enumerate((zero, tile * tall(lo * here + m1 * hi), tile * tall(m0 * hi), zero)):
            rhs[r, 1, 3, :, 128 * n : 128 * n + 128] = part
        high = jnp.broadcast_to(sp_h[3, r : r + 1, 0:1].astype(F32), (16, 128))
        m0 = ((1.0 - high) * (reach * has_upper)).astype(BF16)
        m1 = (high * has_upper).astype(BF16)
        here = jnp.broadcast_to(has_upper, (16, 128)).astype(BF16)
        tile = pe[1 + r, cols + 1]
        for n, part in enumerate((tile * tall(m0 * hi), tile * tall(m1 * hi), tile * tall(lo * here), zero)):
            rhs[r, cols, 4, :, 128 * n : 128 * n + 128] = part
    get_a.wait()

    def sweep(t, carry):
        c = lax.div(t, 2)
        r = lax.rem(slow + lax.rem(t, 2), 2)
        ps_landing(r, c).wait_recv()
        present = jnp.where(r == 0, has_before, has_after)
        here = lo * jnp.broadcast_to(present, (16, 128)).astype(BF16)
        last = []
        for i in range(2):
            g = 2 * c + i
            for odd in range(2):
                y = 2 * g + odd
                tile = pe[3 * r, 1 + y]
                m0 = m0t[3 * r, 1 + y]
                m1 = m1t[3 * r, 1 + y]
                middle = tile * tall(m0 * hi)
                if odd == 0:
                    parts = (tile * tall(here), middle, tile * tall(m1 * hi), zero)
                else:
                    parts = (tile * tall(here + m1 * hi), middle, zero, zero)
                for n, part in enumerate(parts):
                    rhs[r, 1 + y, 1 + r, :, 128 * n : 128 * n + 128] = part
                right = rhs[r, 1 + y].reshape(5 * B, 512)
                left = a_v[r, y]
                made = jnp.dot(left[:, :256], right[:256], preferred_element_type=F32)
                made += jnp.dot(left[:, 256:], right[256:], preferred_element_type=F32)
                made = made.astype(BF16)
                for n, place in enumerate((r, 2, 3 + r, 1 - r)):
                    gs[g, place, r, B * odd : B * odd + B] = made[:, 128 * n : 128 * n + 128]
            right = jnp.concatenate([gs[g, place, r] for place in (r, 2, 3 + r, 1 - r)], axis=1)
            leave = transposed_dot(la[r, g], right)
            for n in range(3):
                msg[r, c, 3 * i + n] = leave[:, 128 * n : 128 * n + 128].astype(BF16)
            last.append(leave[:, 384:512])
        msg[r, c, 6] = jnp.concatenate([last[0][:, :B], last[1][:, :B]], axis=1).astype(BF16)
        ms_copy(r, c).start()
        return carry

    lax.fori_loop(0, 2 * chunks, sweep, 0)

    mg_copies = [
        remote(gr.at[0], gr.at[aggs], mg_send.at[0], mg_recv.at[1], around[2]),
        remote(gl.at[aggs], gl.at[0], mg_send.at[1], mg_recv.at[0], around[3]),
    ]

    def gather(t, carry):
        g = lax.rem(t + aggs - 1, aggs)
        right = jnp.concatenate([gs[g, n].reshape(256, 128) for n in range(5)], axis=1)
        made = transposed_dot(lb[g].reshape(256, 192), right)

        def piece(rows, n):
            return made[B * rows : B * rows + B, 128 * n : 128 * n + 128]

        low = lo32 > 0.5
        um, up, ce, d0, d1 = (swap_halves(piece(0, n)) for n in range(5))
        acc[g, 0] = jnp.where(low, d0, um)
        acc[g, 1] = jnp.where(low, um, 0.0)
        acc[g, 2] = jnp.where(low, 0.0, ce)
        acc[g, 3] = jnp.where(low, ce, d0 + d1)
        acc[g, 4] = jnp.where(low, d1, up)
        acc[g, 5] = jnp.where(low, up, 0.0)
        um, up, ce, d0, d1 = (piece(1, n) for n in range(5))
        gr[g, 0] = jnp.where(low, um, d0).astype(BF16)
        gr[g, 1] = jnp.where(low, up, d1).astype(BF16)
        gr[g, 2] = ce.astype(BF16)
        gr[g, 3] = jnp.where(low, d0 + d1, 0.0).astype(BF16)
        um, up, ce, d0, d1 = (piece(2, n) for n in range(5))
        gl[g + 1, 0] = um.astype(BF16)
        gl[g + 1, 1] = up.astype(BF16)
        gl[g + 1, 2] = ce.astype(BF16)
        gl[g + 1, 3] = (d0 + d1).astype(BF16)

        @pl.when(t == 1)
        def _():
            for copy in mg_copies:
                copy.start()

        return carry

    lax.fori_loop(0, aggs, gather, 0)
    for copy in mg_copies:
        copy.wait_recv()

    def finish(c, carry):
        low = lo32 > 0.5
        ms_landing(1 - slow, c).wait_recv()
        ms_landing(slow, c).wait_recv()
        for i in range(2):
            g = 2 * c + i
            b0, b1, b2 = (rmsg[0, c, 3 * i + n].astype(F32) for n in range(3))
            f0, f1, f2 = (rmsg[1, c, 3 * i + n].astype(F32) for n in range(3))
            b3, f3 = rmsg[0, c, 6].astype(F32), rmsg[1, c, 6].astype(F32)
            if i == 1:
                b3, f3 = swap_halves(b3), swap_halves(f3)
            l0, l1, l2, l3 = (gl[g, n].astype(F32) for n in range(4))
            r0, r1, r2, r3 = (gr[g + 1, n].astype(F32) for n in range(4))
            tiles = (
                (1, jnp.where(low, b3, 0.0)),
                (3, acc[g, 0] + b1 + l0 + jnp.where(low, 0.0, r0)),
                (4, acc[g, 1] + jnp.where(low, b2 + r0, 0.0)),
                (5, acc[g, 2] + l2 + jnp.where(low, 0.0, b2 + f2)),
                (6, acc[g, 3] + b0 + f0 + l3 + r2),
                (7, r3),
                (8, acc[g, 4] + f1 + l1 + jnp.where(low, 0.0, r1)),
                (9, acc[g, 5] + jnp.where(low, f2 + r1, 0.0)),
                (11, jnp.where(low, f3, 0.0)),
            )
            for t, value in tiles:
                out[0, g, :, 128 * t : 128 * t + 128] = value.astype(BF16)
        return carry

    lax.fori_loop(0, chunks, finish, 0)

    for copy in sp_copies + pg_copies + mg_copies:
        copy.wait_send()
    for r in range(2):
        for c in range(chunks):
            ps_copy(r, c).wait_send()
            ms_copy(r, c).wait_send()


def local(a_vals, p_vals, spill_axis):
    n_sub = lax.axis_size("sub")
    n_gy = lax.axis_size("gy")
    cols = a_vals.shape[1]
    aggs = cols // 2
    chunks = aggs // 2
    dma = pltpu.SemaphoreType.DMA
    return pl.pallas_call(
        functools.partial(kernel, n_sub, n_gy, cols),
        out_shape=jax.ShapeDtypeStruct((1, aggs, B, SLOTS * B), BF16),
        in_specs=[pl.BlockSpec(memory_space=pl.ANY)] * 3,
        out_specs=pl.BlockSpec(memory_space=pltpu.VMEM),
        scratch_shapes=[
            pltpu.VMEM((2, cols, B, 5 * B), BF16),
            pltpu.VMEM((4, cols + 2, B, 128), BF16),
            pltpu.VMEM((2, cols), jnp.int32),
            pltpu.VMEM((4, 2, cols), jnp.int32),
            pltpu.VMEM((4, cols + 2, 16, 128), BF16),
            pltpu.VMEM((4, cols + 2, 16, 128), BF16),
            pltpu.VMEM((2, cols + 2, 5, B, 512), BF16),
            pltpu.VMEM((2, aggs, 128, B), BF16),
            pltpu.VMEM((aggs, 2, 128, 192), BF16),
            pltpu.VMEM((aggs, 5, 2, 128, 128), BF16),
            pltpu.VMEM((2, chunks, 7, B, 128), BF16),
            pltpu.VMEM((2, chunks, 7, B, 128), BF16),
            pltpu.VMEM((aggs, 6, B, 128), F32),
            pltpu.VMEM((aggs + 1, 4, B, 128), BF16),
            pltpu.VMEM((aggs + 1, 4, B, 128), BF16),
            dma((3,)),
            dma((4,)),
            dma((4,)),
            dma((2, chunks)),
            dma((2, chunks)),
            dma((2,)),
            dma((2,)),
            dma((2, chunks)),
            dma((2, chunks)),
            dma((2,)),
            dma((2,)),
        ],
        compiler_params=pltpu.CompilerParams(
            collective_id=0, has_side_effects=True, vmem_limit_bytes=48 * 1024 * 1024
        ),
        cost_estimate=pl.CostEstimate(flops=1_300_000_000, bytes_accessed=4_000_000, transcendentals=0),
    )(a_vals, p_vals, spill_axis)


def solution(mesh):
    return jax.shard_map(
        local,
        mesh=mesh,
        in_specs=(P("sub", "gy", None, None), P("sub", "gy", None, None), P("sub", "gy")),
        out_specs=P("sub", "gy", None, None),
        check_vma=False,
    )
```

time: 671 us -> 26.3 us (0.04)
  the two profiles are of different devices: /device:TPU:40 before, /device:TPU:0 now
where the time goes in v1:
time: 26.3 us; the launch traced here: 26.1 us
  Pallas kernels  21.8 us (83%)
  local copies, waits for them, and re-layouts  4.31 us (16%)
    pallas_call x1, Pallas kernels, local(): pl.pallas_call(functools.partial(kernel, n_sub, n_gy, cols), out_shape=ja...  21.8 us
    unnamed x7, local copies, waits for them, and re-layouts  4.31 us

profile of v1, /device:TPU:0, one launch (start us, length us, event | category | flops | bytes accessed | tf_op | source)
XLA Modules:
  0.0 26.1 jit_solution(6525569857493571169)
XLA Ops:
  0.0 0.0 copy-start
  0.0 1.4 %copy-done = bf16[2,16,64,320]{3,2,1,0:T(8,128)(2,1)S(1)} copy-done((bf16[2,16,64,320]{3,2,1,0:T(8,128)(2,1)S(1)}, bf16[2,16,64,320]{3,2,1,0:T(8,128)(2,1)}, u32[]{:S(2)}) %copy-start) | copy-done | bytes 1310744
  1.4 0.0 copy-start.1
  1.4 1.0 %copy-done.1 = bf16[2,16,64,128]{3,2,1,0:T(8,128)(2,1)S(1)} copy-done((bf16[2,16,64,128]{3,2,1,0:T(8,128)(2,1)S(1)}, bf16[2,16,64,128]{3,2,1,0:T(8,128)(2,1)}, u32[]{:S(2)}) %copy-start.1) | copy-done | bytes 524312
  2.5 0.0 copy-start.2
  2.5 0.7 %copy-done.2 = s32[2,16]{1,0:T(2,128)S(1)} copy-done((s32[2,16]{1,0:T(2,128)S(1)}, s32[2,16]{1,0:T(2,128)}, u32[]{:S(2)}) %copy-start.2) | copy-done | bytes 152
  3.1 21.8 %shard_map.37 = bf16[1,8,64,1600]{3,2,1,0:T(8,128)(2,1)S(1)} custom-call(bf16[2,16,64,320]{3,2,1,0:T(8,128)(2,1)S(1)} %copy-done, bf16[2,16,64,128]{3,2,1,0:T(8,128)(2,1)S(1)} %copy-done.1, s32[2,16]{1,0:T(2,128)S(1)} %copy-done.2), custom_call_target="tpu_custom_call" | custom-call | flops 1300000000 | bytes 4000000 | tf_op jit(solution)/shard_map/pallas_call | solution.py:340
  24.9 1.2 %copy.5 = bf16[1,8,64,1600]{3,2,1,0:T(8,128)(2,1)} copy(bf16[1,8,64,1600]{3,2,1,0:T(8,128)(2,1)S(1)} %shard_map.37) | data formatting | bytes 3276800
Async XLA Ops:
  0.0 1.4 %copy-start = (bf16[2,16,64,320]{3,2,1,0:T(8,128)(2,1)S(1)}, bf16[2,16,64,320]{3,2,1,0:T(8,128)(2,1)}, u32[]{:S(2)}) copy-start(bf16[2,16,64,320]{3,2,1,0:T(8,128)(2,1)} %a_hbm.1) | copy-start | bytes 3932164
  1.4 1.0 %copy-start.1 = (bf16[2,16,64,128]{3,2,1,0:T(8,128)(2,1)S(1)}, bf16[2,16,64,128]{3,2,1,0:T(8,128)(2,1)}, u32[]{:S(2)}) copy-start(bf16[2,16,64,128]{3,2,1,0:T(8,128)(2,1)} %p_hbm.1) | copy-start | bytes 1572868
  2.5 0.7 %copy-start.2 = (s32[2,16]{1,0:T(2,128)S(1)}, s32[2,16]{1,0:T(2,128)}, u32[]{:S(2)}) copy-start(s32[2,16]{1,0:T(2,128)} %sp_hbm.1) | copy-start | bytes 388

commit v2 on v1

v2 whole, which is shorter than its diff:
```python
import functools

import jax
import jax.numpy as jnp
from jax import lax
from jax.experimental import pallas as pl
from jax.experimental.pallas import tpu as pltpu
from jax.sharding import PartitionSpec as P

MESH = pl.DeviceIdType.MESH
F32 = jnp.float32
BF16 = jnp.bfloat16
B = 64
SLOTS = 25


def lanes_low(rows, dtype):
    lane = lax.broadcasted_iota(jnp.int32, (rows, 128), 1)
    return jnp.where(lane < B, 1.0, 0.0).astype(dtype)


def swap_halves(tile):
    return jnp.concatenate([tile[:, B:], tile[:, :B]], axis=1)


def tall(mask):
    return jnp.concatenate([mask] * 4, axis=0)


def spread(row, cols):
    wide = jnp.broadcast_to(row, (cols, cols))
    at = lax.broadcasted_iota(jnp.int32, (cols, cols), 0)
    lane = lax.broadcasted_iota(jnp.int32, (cols, cols), 1)
    column = jnp.sum(jnp.where(at == lane, wide, 0.0), axis=1, keepdims=True)
    column = jnp.broadcast_to(column, (cols, 128))
    return jnp.broadcast_to(column[:, None, :], (cols, 16, 128)).astype(BF16)


def beside(tiles):
    return jnp.concatenate(tiles, axis=1)


def below(tiles):
    return jnp.concatenate(tiles, axis=0)


def kernel(
    n_sub, n_gy, cols,
    a_hbm, p_hbm, sp_hbm, out,
    a_v, pe, sp_own, sp_h, m0t, m1t, turn, flip, gs, msg, rmsg, acc, gl, gr,
    local_sem, sp_send, sp_recv, ps_send, ps_recv, pg_send, pg_recv,
    ms_send, ms_recv, mg_send, mg_recv,
):
    s = lax.axis_index("sub")
    z = lax.axis_index("gy")
    aggs = cols // 2
    chunks = aggs // 2
    around = (
        (lax.rem(s + n_sub - 1, n_sub), z),
        (lax.rem(s + 1, n_sub), z),
        (s, lax.rem(z + n_gy - 1, n_gy)),
        (s, lax.rem(z + 1, n_gy)),
    )
    there = (s > 0, s < n_sub - 1, z > 0, z < n_gy - 1)
    slow = lax.rem(s, 2)

    barrier = pltpu.get_barrier_semaphore()
    for d in range(4):

        @pl.when(there[d])
        def _():
            pl.semaphore_signal(barrier, inc=1, device_id=around[d], device_id_type=MESH)

    get_sp = pltpu.make_async_copy(sp_hbm, sp_own, local_sem.at[0])
    get_p = pltpu.make_async_copy(p_hbm, pe.at[1:3, 1 : cols + 1], local_sem.at[1])
    get_a = pltpu.make_async_copy(a_hbm, a_v, local_sem.at[2])
    get_sp.start()
    get_p.start()
    get_a.start()
    ones = [jnp.where(t, 1, 0).astype(jnp.int32) for t in there]
    pl.semaphore_wait(barrier, ones[0] + ones[1] + ones[2] + ones[3])

    def remote(src, dst, send, recv, device):
        return pltpu.make_async_remote_copy(
            src_ref=src, dst_ref=dst, send_sem=send, recv_sem=recv, device_id=device, device_id_type=MESH
        )

    def sp_copy(d, landing=False):
        e = d if landing else d ^ 1
        return remote(sp_hbm, sp_h.at[e], sp_send.at[d], sp_recv.at[e], around[d])

    def pg_copy(d, landing=False):
        e = d if landing else d ^ 1
        return remote(
            p_hbm.at[:, (cols - 1) * (d - 2)], pe.at[1:3, (cols + 1) * (e - 2)],
            pg_send.at[d - 2], pg_recv.at[e - 2], around[d],
        )

    def ps_copy(d, c, landing=False):
        e = d if landing else d ^ 1
        return remote(
            p_hbm.at[d, pl.ds(4 * c, 4)], pe.at[3 * e, pl.ds(1 + 4 * c, 4)],
            ps_send.at[d, c], ps_recv.at[e, c], around[d],
        )

    def ms_copy(d, c, landing=False):
        e = d if landing else d ^ 1
        return remote(msg.at[d, c], rmsg.at[e, c], ms_send.at[d, c], ms_recv.at[e, c], around[d])

    mg_copies = {
        2: remote(gr.at[0], gr.at[aggs], mg_send.at[0], mg_recv.at[1], around[2]),
        3: remote(gl.at[aggs], gl.at[0], mg_send.at[1], mg_recv.at[0], around[3]),
    }
    mg_landing = {
        2: remote(gl.at[aggs], gl.at[0], mg_send.at[0], mg_recv.at[0], around[2]),
        3: remote(gr.at[0], gr.at[aggs], mg_send.at[1], mg_recv.at[1], around[3]),
    }

    for d in range(4):

        @pl.when(there[d])
        def _():
            sp_copy(d).start()

    for d in (2, 3):

        @pl.when(there[d])
        def _():
            pg_copy(d).start()

    for d in (0, 1):

        @pl.when(there[d])
        def _():
            for c in range(chunks):
                ps_copy(d, c).start()

    tile0 = jnp.zeros((B, 128), BF16)
    for d in range(4):

        @pl.when(jnp.logical_not(there[d]))
        def _():
            sp_h[d] = jnp.zeros((2, cols), jnp.int32)
            if d < 2:
                for y in range(cols):
                    pe[3 * d, 1 + y] = tile0
                for c in range(chunks):
                    for n in range(7):
                        rmsg[d, c, n] = tile0
            else:
                for r in range(2):
                    pe[1 + r, (cols + 1) * (d - 2)] = tile0
                for n in range(4):
                    if d == 2:
                        gl[0, n] = tile0
                    else:
                        gr[aggs, n] = tile0

    lo = lanes_low(16, BF16)
    hi = (1.0 - lanes_low(16, F32)).astype(BF16)
    lo32 = lanes_low(B, F32)

    def flag(condition, rows=16):
        return jnp.broadcast_to(jnp.where(condition, 1.0, 0.0).astype(F32), (rows, 128)).astype(BF16)

    reach = (flag(there[0]), flag(there[1]))
    side = (flag(there[2]), flag(there[3]))

    for g in range(aggs):
        for t in (0, 2, 10):
            out[0, g, :, 128 * t : 128 * t + 128] = tile0
        out[0, g, :, 1536:] = jnp.zeros((B, B), BF16)
        gs[g, 4, 0] = jnp.zeros((128, 128), BF16)
        gs[g, 3, 1] = jnp.zeros((128, 128), BF16)

    def masks_of_row(row, e):
        spill = spread(row, cols)
        straight = 1.0 - spill
        m0t[e, 1 : cols + 1] = straight if e in (0, 3) else straight * reach[e - 1][None]
        m1t[e, 2:cols] = spill[1 : cols - 1]
        m1t[e, 1] = spill[0] * side[0]
        m1t[e, cols] = spill[cols - 1] * side[1]

    get_sp.wait()
    own = sp_own[...].astype(F32)
    masks_of_row(own[0:1], 1)
    masks_of_row(own[1:2], 2)
    get_p.wait()

    def prepare(t, carry):
        for r in range(2):
            pair = []
            for odd in range(2):
                y = 2 * t + odd
                tile = pe[1 + r, 1 + y]
                turn[r, y] = swap_halves(tile)
                pair.append(tile)
            flip[r, t] = below(pair).T
        return carry

    lax.fori_loop(0, aggs, prepare, 0)

    for d in range(4):

        @pl.when(there[d])
        def _():
            sp_copy(d, True).wait_recv()

    masks_of_row(sp_h[0, 1:2].astype(F32), 0)
    masks_of_row(sp_h[1, 0:1].astype(F32), 3)
    for d, at, column in ((2, 0, cols - 1), (3, cols + 1, 0)):
        for r in range(2):
            spill = jnp.broadcast_to(sp_h[d, r : r + 1, column : column + 1].astype(F32), (16, 128)).astype(BF16)
            m0t[1 + r, at] = (1.0 - spill) * reach[r]
            m1t[1 + r, at] = spill

    for d in (2, 3):

        @pl.when(there[d])
        def _():
            pg_copy(d, True).wait_recv()

    get_a.wait()

    def inner(r, y, odd):
        tile = turn[r, y]
        m0, m1 = m0t[1 + r, 1 + y], m1t[1 + r, 1 + y]
        first = tile * tall(m0 * lo)
        if odd == 0:
            return first, tile * tall(m1 * lo + hi), tile0
        return first, tile * tall(hi), tile * tall(m1 * lo)

    def sweep(r, c):
        @pl.when(there[r])
        def _():
            ps_copy(r, c, True).wait_recv()

        last = []
        for i in range(2):
            g = 2 * c + i
            own = [inner(r, 2 * g + odd, odd) for odd in range(2)]
            made = []
            for odd in range(2):
                y = 2 * g + odd
                first, second, third = inner(1 - r, y, odd)
                x_in = beside([tile0, second, third, first])
                tile = pe[3 * r, 1 + y]
                m0, m1 = m0t[3 * r, 1 + y], m1t[3 * r, 1 + y]
                middle = tile * tall(m0 * hi)
                if odd == 0:
                    x_out = beside([tile * tall(lo), middle, tile * tall(m1 * hi), tile0])
                else:
                    x_out = beside([tile * tall(lo + m1 * hi), middle, tile0, tile0])
                at = y - 1 + 2 * odd
                tile = pe[1 + r, 1 + at]
                m0, m1 = m0t[1 + r, 1 + at], m1t[1 + r, 1 + at]
                if odd == 0:
                    y_out = beside([tile0, tile * tall(lo + m1 * hi), tile * tall(m0 * hi), tile0])
                else:
                    y_out = beside([tile * tall(m0 * hi), tile * tall(m1 * hi), tile * tall(lo), tile0])
                y_in = beside([*own[1 - odd], tile0])
                blocks = [beside([*own[odd], tile0])]
                blocks += [x_out, x_in] if r == 0 else [x_in, x_out]
                blocks += [y_out, y_in] if odd == 0 else [y_in, y_out]
                left = a_v[r, y]
                value = jnp.dot(left[:, :256], below(blocks[:4]), preferred_element_type=F32)
                value += jnp.dot(left[:, 256:], blocks[4], preferred_element_type=F32)
                made.append(value.astype(BF16))
            right = below(made)
            m0 = [m0t[1 + r, 1 + 2 * g + odd] for odd in range(2)]
            leave = jnp.dot(
                flip[r, g, B:] * tall(m0[0] * lo + m0[1] * hi), right, preferred_element_type=F32
            )
            for n, place in enumerate((r, 2, 3 + r, 1 - r)):
                gs[g, place, r] = right[:, 128 * n : 128 * n + 128]
            for n in range(3):
                msg[r, c, 3 * i + n] = leave[:, 128 * n : 128 * n + 128].astype(BF16)
            last.append(leave[:, 384:512])
        msg[r, c, 6] = beside([last[0][:, :B], last[1][:, :B]]).astype(BF16)

        @pl.when(there[r])
        def _():
            ms_copy(r, c).start()

    for behind in range(2):

        @pl.when(slow == behind)
        def _():
            def step(c, carry):
                sweep(1 - behind, c)
                sweep(behind, c)
                return carry

            lax.fori_loop(0, chunks, step, 0)

    low = lo32 > 0.5

    def gather(t, carry):
        g = lax.rem(t + aggs - 1, aggs)
        right = beside([gs[g, n].reshape(256, 128) for n in range(5)])
        m1 = [[m1t[1 + r, 1 + 2 * g + odd] for odd in range(2)] for r in range(2)]
        left = below([
            beside([flip[r, g, :B] for r in range(2)]),
            beside([flip[r, g, B:] * tall(m1[r][0] * lo) for r in range(2)]),
            beside([flip[r, g, B:] * tall(m1[r][1] * hi) for r in range(2)]),
        ])
        made = jnp.dot(left, right, preferred_element_type=F32)

        def piece(rows, n):
            return made[B * rows : B * rows + B, 128 * n : 128 * n + 128]

        um, up, ce, d0, d1 = (swap_halves(piece(0, n)) for n in range(5))
        acc[g, 0] = jnp.where(low, d0, um)
        acc[g, 1] = jnp.where(low, um, 0.0)
        acc[g, 2] = jnp.where(low, 0.0, ce)
        acc[g, 3] = jnp.where(low, ce, d0 + d1)
        acc[g, 4] = jnp.where(low, d1, up)
        acc[g, 5] = jnp.where(low, up, 0.0)
        um, up, ce, d0, d1 = (piece(1, n) for n in range(5))
        gr[g, 0] = jnp.where(low, um, d0).astype(BF16)
        gr[g, 1] = jnp.where(low, up, d1).astype(BF16)
        gr[g, 2] = ce.astype(BF16)
        gr[g, 3] = jnp.where(low, d0 + d1, 0.0).astype(BF16)
        um, up, ce, d0, d1 = (piece(2, n) for n in range(5))
        gl[g + 1, 0] = um.astype(BF16)
        gl[g + 1, 1] = up.astype(BF16)
        gl[g + 1, 2] = ce.astype(BF16)
        gl[g + 1, 3] = (d0 + d1).astype(BF16)

        @pl.when(t == 1)
        def _():
            for d in (2, 3):

                @pl.when(there[d])
                def _():
                    mg_copies[d].start()

        return carry

    lax.fori_loop(0, aggs, gather, 0)
    for d in (2, 3):

        @pl.when(there[d])
        def _():
            mg_landing[d].wait_recv()

    def finish(c, carry):
        for d in range(2):

            @pl.when(there[d])
            def _():
                ms_copy(d, c, True).wait_recv()

        for i in range(2):
            g = 2 * c + i
            b0, b1, b2 = (rmsg[0, c, 3 * i + n].astype(F32) for n in range(3))
            f0, f1, f2 = (rmsg[1, c, 3 * i + n].astype(F32) for n in range(3))
            b3, f3 = rmsg[0, c, 6].astype(F32), rmsg[1, c, 6].astype(F32)
            if i == 1:
                b3, f3 = swap_halves(b3), swap_halves(f3)
            l0, l1, l2, l3 = (gl[g, n].astype(F32) for n in range(4))
            r0, r1, r2, r3 = (gr[g + 1, n].astype(F32) for n in range(4))
            tiles = (
                (1, jnp.where(low, b3, 0.0)),
                (3, acc[g, 0] + b1 + l0 + jnp.where(low, 0.0, r0)),
                (4, acc[g, 1] + jnp.where(low, b2 + r0, 0.0)),
                (5, acc[g, 2] + l2 + jnp.where(low, 0.0, b2 + f2)),
                (6, acc[g, 3] + b0 + f0 + l3 + r2),
                (7, r3),
                (8, acc[g, 4] + f1 + l1 + jnp.where(low, 0.0, r1)),
                (9, acc[g, 5] + jnp.where(low, f2 + r1, 0.0)),
                (11, jnp.where(low, f3, 0.0)),
            )
            for t, value in tiles:
                out[0, g, :, 128 * t : 128 * t + 128] = value.astype(BF16)
        return carry

    lax.fori_loop(0, chunks, finish, 0)

    for d in range(4):

        @pl.when(there[d])
        def _():
            sp_copy(d).wait_send()
            if d < 2:
                for c in range(chunks):
                    ps_copy(d, c).wait_send()
                    ms_copy(d, c).wait_send()
            else:
                pg_copy(d).wait_send()
                mg_copies[d].wait_send()


def local(a_vals, p_vals, spill_axis):
    n_sub = lax.axis_size("sub")
    n_gy = lax.axis_size("gy")
    cols = a_vals.shape[1]
    aggs = cols // 2
    chunks = aggs // 2
    dma = pltpu.SemaphoreType.DMA
    return pl.pallas_call(
        functools.partial(kernel, n_sub, n_gy, cols),
        out_shape=jax.ShapeDtypeStruct((1, aggs, B, SLOTS * B), BF16),
        in_specs=[pl.BlockSpec(memory_space=pl.ANY)] * 3,
        out_specs=pl.BlockSpec(memory_space=pltpu.VMEM),
        scratch_shapes=[
            pltpu.VMEM((2, cols, B, 5 * B), BF16),
            pltpu.VMEM((4, cols + 2, B, 128), BF16),
            pltpu.VMEM((2, cols), jnp.int32),
            pltpu.VMEM((4, 2, cols), jnp.int32),
            pltpu.VMEM((4, cols + 2, 16, 128), BF16),
            pltpu.VMEM((4, cols + 2, 16, 128), BF16),
            pltpu.VMEM((2, cols, B, 128), BF16),
            pltpu.VMEM((2, aggs, 128, 128), BF16),
            pltpu.VMEM((aggs, 5, 2, 128, 128), BF16),
            pltpu.VMEM((2, chunks, 7, B, 128), BF16),
            pltpu.VMEM((2, chunks, 7, B, 128), BF16),
            pltpu.VMEM((aggs, 6, B, 128), F32),
            pltpu.VMEM((aggs + 1, 4, B, 128), BF16),
            pltpu.VMEM((aggs + 1, 4, B, 128), BF16),
            dma((3,)),
            dma((4,)),
            dma((4,)),
            dma((2, chunks)),
            dma((2, chunks)),
            dma((2,)),
            dma((2,)),
            dma((2, chunks)),
            dma((2, chunks)),
            dma((2,)),
            dma((2,)),
        ],
        compiler_params=pltpu.CompilerParams(
            collective_id=0, has_side_effects=True, vmem_limit_bytes=40 * 1024 * 1024
        ),
        cost_estimate=pl.CostEstimate(flops=1_300_000_000, bytes_accessed=4_000_000, transcendentals=0),
    )(*(pltpu.with_memory_space_constraint(x, pltpu.HBM) for x in (a_vals, p_vals, spill_axis)))


def solution(mesh):
    return jax.shard_map(
        local,
        mesh=mesh,
        in_specs=(P("sub", "gy", None, None), P("sub", "gy", None, None), P("sub", "gy")),
        out_specs=P("sub", "gy", None, None),
        check_vma=False,
    )
```

time: 26.3 us -> 19 us (0.72)
  the two profiles are of different devices: /device:TPU:0 before, /device:TPU:24 now
where the time goes in v2:
time: 19 us; the launch traced here: 18.9 us
  Pallas kernels  17.7 us (93%)
  local copies, waits for them, and re-layouts  1.19 us (6%)
    pallas_call x1, Pallas kernels, local(): pl.pallas_call(functools.partial(kernel, n_sub, n_gy, cols), out_shape=ja...  17.7 us
    unnamed x1, local copies, waits for them, and re-layouts  1.19 us

profile of v2, /device:TPU:24, one launch (start us, length us, event | category | flops | bytes accessed | tf_op | source)
XLA Modules:
  0.0 18.9 jit_solution(13545618175309422727)
XLA Ops:
  0.0 17.7 %shard_map.37 = bf16[1,8,64,1600]{3,2,1,0:T(8,128)(2,1)S(1)} custom-call(bf16[2,16,64,320]{3,2,1,0:T(8,128)(2,1)} %a_hbm.1, bf16[2,16,64,128]{3,2,1,0:T(8,128)(2,1)} %p_hbm.1, s32[2,16]{1,0:T(2,128)} %sp_hbm.1), custom_call_target="tpu_custom_call" | custom-call | flops 1300000000 | bytes 4000000 | tf_op jit(solution)/shard_map/pallas_call | solution.py:401
  17.7 1.2 %copy.5 = bf16[1,8,64,1600]{3,2,1,0:T(8,128)(2,1)} copy(bf16[1,8,64,1600]{3,2,1,0:T(8,128)(2,1)S(1)} %shard_map.37) | data formatting | bytes 3276800

commit v3 on v2

--- a/solution.py
+++ b/solution.py
@@ -47,7 +47,7 @@
 def kernel(
     n_sub, n_gy, cols,
     a_hbm, p_hbm, sp_hbm, out,
-    a_v, pe, sp_own, sp_h, m0t, m1t, turn, flip, gs, msg, rmsg, acc, gl, gr,
+    a_v, pe, sp_own, sp_h, m0t, m1t, turn, flip, part, gs, msg, rmsg, acc, gl, gr,
     local_sem, sp_send, sp_recv, ps_send, ps_recv, pg_send, pg_recv,
     ms_send, ms_recv, mg_send, mg_recv,
 ):
@@ -63,6 +63,7 @@
     )
     there = (s > 0, s < n_sub - 1, z > 0, z < n_gy - 1)
     slow = lax.rem(s, 2)
+    order = [0, chunks - 1, *range(1, chunks - 1)]
 
     barrier = pltpu.get_barrier_semaphore()
     for d in range(4):
@@ -77,6 +78,8 @@
     get_sp.start()
     get_p.start()
     get_a.start()
+    get_sp.wait()
+    get_p.wait()
     ones = [jnp.where(t, 1, 0).astype(jnp.int32) for t in there]
     pl.semaphore_wait(barrier, ones[0] + ones[1] + ones[2] + ones[3])
 
@@ -87,25 +90,29 @@
 
     def sp_copy(d, landing=False):
         e = d if landing else d ^ 1
-        return remote(sp_hbm, sp_h.at[e], sp_send.at[d], sp_recv.at[e], around[d])
+        return remote(sp_own, sp_h.at[e], sp_send.at[d], sp_recv.at[e], around[d])
 
     def pg_copy(d, landing=False):
         e = d if landing else d ^ 1
         return remote(
-            p_hbm.at[:, (cols - 1) * (d - 2)], pe.at[1:3, (cols + 1) * (e - 2)],
+            pe.at[1:3, 1 + (cols - 1) * (d - 2)], pe.at[1:3, (cols + 1) * (e - 2)],
             pg_send.at[d - 2], pg_recv.at[e - 2], around[d],
         )
 
     def ps_copy(d, c, landing=False):
         e = d if landing else d ^ 1
         return remote(
-            p_hbm.at[d, pl.ds(4 * c, 4)], pe.at[3 * e, pl.ds(1 + 4 * c, 4)],
+            pe.at[1 + d, pl.ds(1 + 4 * c, 4)], pe.at[3 * e, pl.ds(1 + 4 * c, 4)],
             ps_send.at[d, c], ps_recv.at[e, c], around[d],
         )
 
-    def ms_copy(d, c, landing=False):
+    def ms_copy(d, c, late, landing=False):
         e = d if landing else d ^ 1
-        return remote(msg.at[d, c], rmsg.at[e, c], ms_send.at[d, c], ms_recv.at[e, c], around[d])
+        tiles = pl.ds(3, 4) if late else pl.ds(0, 3)
+        return remote(
+            msg.at[d, c, tiles], rmsg.at[e, c, tiles],
+            ms_send.at[d, c, late], ms_recv.at[e, c, late], around[d],
+        )
 
     mg_copies = {
         2: remote(gr.at[0], gr.at[aggs], mg_send.at[0], mg_recv.at[1], around[2]),
@@ -116,24 +123,37 @@
         3: remote(gr.at[0], gr.at[aggs], mg_send.at[1], mg_recv.at[1], around[3]),
     }
 
+    for behind in range(2):
+
+        @pl.when(jnp.logical_and(slow == behind, there[behind]))
+        def _():
+            ps_copy(behind, 0).start()
+
     for d in range(4):
 
         @pl.when(there[d])
         def _():
             sp_copy(d).start()
 
+    for behind in range(2):
+
+        @pl.when(jnp.logical_and(slow == behind, there[behind]))
+        def _():
+            for c in order[1:]:
+                ps_copy(behind, c).start()
+
     for d in (2, 3):
 
         @pl.when(there[d])
         def _():
             pg_copy(d).start()
 
-    for d in (0, 1):
-
-        @pl.when(there[d])
-        def _():
-            for c in range(chunks):
-                ps_copy(d, c).start()
+    for behind in range(2):
+
+        @pl.when(jnp.logical_and(slow == 1 - behind, there[behind]))
+        def _():
+            for c in order:
+                ps_copy(behind, c).start()
 
     tile0 = jnp.zeros((B, 128), BF16)
     for d in range(4):
@@ -158,7 +178,7 @@
 
     lo = lanes_low(16, BF16)
     hi = (1.0 - lanes_low(16, F32)).astype(BF16)
-    lo32 = lanes_low(B, F32)
+    low = lanes_low(B, F32) > 0.5
 
     def flag(condition, rows=16):
         return jnp.broadcast_to(jnp.where(condition, 1.0, 0.0).astype(F32), (rows, 128)).astype(BF16)
@@ -181,11 +201,9 @@
         m1t[e, 1] = spill[0] * side[0]
         m1t[e, cols] = spill[cols - 1] * side[1]
 
-    get_sp.wait()
     own = sp_own[...].astype(F32)
     masks_of_row(own[0:1], 1)
     masks_of_row(own[1:2], 2)
-    get_p.wait()
 
     def prepare(t, carry):
         for r in range(2):
@@ -200,26 +218,6 @@
 
     lax.fori_loop(0, aggs, prepare, 0)
 
-    for d in range(4):
-
-        @pl.when(there[d])
-        def _():
-            sp_copy(d, True).wait_recv()
-
-    masks_of_row(sp_h[0, 1:2].astype(F32), 0)
-    masks_of_row(sp_h[1, 0:1].astype(F32), 3)
-    for d, at, column in ((2, 0, cols - 1), (3, cols + 1, 0)):
-        for r in range(2):
-            spill = jnp.broadcast_to(sp_h[d, r : r + 1, column : column + 1].astype(F32), (16, 128)).astype(BF16)
-            m0t[1 + r, at] = (1.0 - spill) * reach[r]
-            m1t[1 + r, at] = spill
-
-    for d in (2, 3):
-
-        @pl.when(there[d])
-        def _():
-            pg_copy(d, True).wait_recv()
-
     get_a.wait()
 
     def inner(r, y, odd):
@@ -230,27 +228,19 @@
             return first, tile * tall(m1 * lo + hi), tile0
         return first, tile * tall(hi), tile * tall(m1 * lo)
 
-    def sweep(r, c):
-        @pl.when(there[r])
-        def _():
-            ps_copy(r, c, True).wait_recv()
-
-        last = []
+    def keep(r, g):
+        m0 = [m0t[1 + r, 1 + 2 * g + odd] for odd in range(2)]
+        return flip[r, g, B:] * tall(m0[0] * lo + m0[1] * hi)
+
+    def first_rows(r, c):
+        values = []
         for i in range(2):
             g = 2 * c + i
             own = [inner(r, 2 * g + odd, odd) for odd in range(2)]
-            made = []
             for odd in range(2):
                 y = 2 * g + odd
                 first, second, third = inner(1 - r, y, odd)
                 x_in = beside([tile0, second, third, first])
-                tile = pe[3 * r, 1 + y]
-                m0, m1 = m0t[3 * r, 1 + y], m1t[3 * r, 1 + y]
-                middle = tile * tall(m0 * hi)
-                if odd == 0:
-                    x_out = beside([tile * tall(lo), middle, tile * tall(m1 * hi), tile0])
-                else:
-                    x_out = beside([tile * tall(lo + m1 * hi), middle, tile0, tile0])
                 at = y - 1 + 2 * odd
                 tile = pe[1 + r, 1 + at]
                 m0, m1 = m0t[1 + r, 1 + at], m1t[1 + r, 1 + at]
@@ -259,44 +249,122 @@
                 else:
                     y_out = beside([tile * tall(m0 * hi), tile * tall(m1 * hi), tile * tall(lo), tile0])
                 y_in = beside([*own[1 - odd], tile0])
+                x_out = beside([tile0] * 4)
                 blocks = [beside([*own[odd], tile0])]
                 blocks += [x_out, x_in] if r == 0 else [x_in, x_out]
                 blocks += [y_out, y_in] if odd == 0 else [y_in, y_out]
                 left = a_v[r, y]
                 value = jnp.dot(left[:, :256], below(blocks[:4]), preferred_element_type=F32)
                 value += jnp.dot(left[:, 256:], blocks[4], preferred_element_type=F32)
-                made.append(value.astype(BF16))
-            right = below(made)
-            m0 = [m0t[1 + r, 1 + 2 * g + odd] for odd in range(2)]
-            leave = jnp.dot(
-                flip[r, g, B:] * tall(m0[0] * lo + m0[1] * hi), right, preferred_element_type=F32
-            )
-            for n, place in enumerate((r, 2, 3 + r, 1 - r)):
-                gs[g, place, r] = right[:, 128 * n : 128 * n + 128]
-            for n in range(3):
-                msg[r, c, 3 * i + n] = leave[:, 128 * n : 128 * n + 128].astype(BF16)
-            last.append(leave[:, 384:512])
-        msg[r, c, 6] = beside([last[0][:, :B], last[1][:, :B]]).astype(BF16)
-
-        @pl.when(there[r])
-        def _():
-            ms_copy(r, c).start()
-
-    for behind in range(2):
-
-        @pl.when(slow == behind)
-        def _():
-            def step(c, carry):
-                sweep(1 - behind, c)
-                sweep(behind, c)
-                return carry
-
-            lax.fori_loop(0, chunks, step, 0)
-
-    low = lo32 > 0.5
-
-    def gather(t, carry):
-        g = lax.rem(t + aggs - 1, aggs)
+                values.append(value)
+        return values
+
+    def first_step(c):
+        values = [first_rows(r, c) for r in range(2)]
+        leave = {}
+        for r in range(2):
+            for i in range(2):
+                pair = below([v[:, 128:].astype(BF16) for v in values[r][2 * i : 2 * i + 2]])
+                leave[r, i] = jnp.dot(keep(r, 2 * c + i), pair, preferred_element_type=F32)
+        for r in range(2):
+            for i in range(2):
+                for odd in range(2):
+                    value = values[r][2 * i + odd]
+                    part[r, 4 * c + 2 * i + odd] = value[:, :384]
+                    gs[2 * c + i, 1 - r, r, B * odd : B * odd + B] = value[:, 384:].astype(BF16)
+                msg[r, c, i] = beside([leave[r, i][:, :B], leave[r, i][:, 128 : 128 + B]]).astype(BF16)
+            msg[r, c, 2] = beside([leave[r, i][:, 256 : 256 + B] for i in range(2)]).astype(BF16)
+        depart(c, 0)
+
+    def last_rows(r, c):
+        made = []
+        for i in range(2):
+            for odd in range(2):
+                y = 4 * c + 2 * i + odd
+                tile = pe[3 * r, 1 + y]
+                m0, m1 = m0t[3 * r, 1 + y], m1t[3 * r, 1 + y]
+                middle = tile * tall(m0 * hi)
+                if odd == 0:
+                    x_out = beside([tile * tall(lo), middle, tile * tall(m1 * hi)])
+                else:
+                    x_out = beside([tile * tall(lo + m1 * hi), middle, tile0])
+                none = beside([tile0] * 3)
+                left = a_v[r, y, :, :128] if r == 0 else a_v[r, y, :, 128:256]
+                right = below([none, x_out] if r == 0 else [x_out, none])
+                value = jnp.dot(left, right, preferred_element_type=F32)
+                made.append((part[r, y] + value).astype(BF16))
+        return made
+
+    def last_step(c):
+        for r in range(2):
+
+            @pl.when(there[r])
+            def _():
+                ps_copy(r, c, True).wait_recv()
+
+        made = [last_rows(r, c) for r in range(2)]
+        leave = {}
+        for r in range(2):
+            for i in range(2):
+                leave[r, i] = jnp.dot(
+                    keep(r, 2 * c + i), below(made[r][2 * i : 2 * i + 2]), preferred_element_type=F32
+                )
+        for r in range(2):
+            for i in range(2):
+                for n, place in enumerate((r, 2, 3 + r)):
+                    for odd in range(2):
+                        gs[2 * c + i, place, r, B * odd : B * odd + B] = made[r][2 * i + odd][:, 128 * n : 128 * n + 128]
+                msg[r, c, 3 + 2 * i] = leave[r, i][:, :128].astype(BF16)
+                msg[r, c, 4 + 2 * i] = beside([leave[r, i][:, 128 + B : 256], leave[r, i][:, 256 + B :]]).astype(BF16)
+        depart(c, 1)
+
+    def depart(c, late):
+        @pl.when(jnp.logical_and(slow == 1, there[1]))
+        def _():
+            ms_copy(1, c, late).start()
+
+        @pl.when(there[0])
+        def _():
+            ms_copy(0, c, late).start()
+
+        @pl.when(jnp.logical_and(slow == 0, there[1]))
+        def _():
+            ms_copy(1, c, late).start()
+
+    def middle_step(c, carry):
+        first_step(c)
+        return carry
+
+    lax.fori_loop(1, chunks - 1, middle_step, 0)
+
+    for d in range(4):
+
+        @pl.when(there[d])
+        def _():
+            sp_copy(d, True).wait_recv()
+
+    masks_of_row(sp_h[0, 1:2].astype(F32), 0)
+    masks_of_row(sp_h[1, 0:1].astype(F32), 3)
+    for d, at, column in ((2, 0, cols - 1), (3, cols + 1, 0)):
+        for r in range(2):
+            spill = jnp.broadcast_to(sp_h[d, r : r + 1, column : column + 1].astype(F32), (16, 128)).astype(BF16)
+            m0t[1 + r, at] = (1.0 - spill) * reach[r]
+            m1t[1 + r, at] = spill
+
+    for d in (2, 3):
+
+        @pl.when(there[d])
+        def _():
+            pg_copy(d, True).wait_recv()
+
+    def end_step(t, carry):
+        first_step(t * (chunks - 1))
+        return carry
+
+    lax.fori_loop(0, 2, end_step, 0)
+
+
+    def gather(g):
         right = beside([gs[g, n].reshape(256, 128) for n in range(5)])
         m1 = [[m1t[1 + r, 1 + 2 * g + odd] for odd in range(2)] for r in range(2)]
         left = below([
@@ -304,8 +372,9 @@
             beside([flip[r, g, B:] * tall(m1[r][0] * lo) for r in range(2)]),
             beside([flip[r, g, B:] * tall(m1[r][1] * hi) for r in range(2)]),
         ])
-        made = jnp.dot(left, right, preferred_element_type=F32)
-
+        return jnp.dot(left, right, preferred_element_type=F32)
+
+    def spread_out(g, made):
         def piece(rows, n):
             return made[B * rows : B * rows + B, 128 * n : 128 * n + 128]
 
@@ -327,9 +396,13 @@
         gl[g + 1, 2] = ce.astype(BF16)
         gl[g + 1, 3] = (d0 + d1).astype(BF16)
 
-        @pl.when(t == 1)
-        def _():
-            for d in (2, 3):
+    def late_step(t, carry):
+        last_step(jnp.where(t == 0, 0, jnp.where(t == 1, chunks - 1, t - 1)))
+        for d, at in ((2, 0), (3, aggs - 1)):
+
+            @pl.when(t == d - 2)
+            def _():
+                spread_out(at, gather(at))
 
                 @pl.when(there[d])
                 def _():
@@ -337,27 +410,39 @@
 
         return carry
 
-    lax.fori_loop(0, aggs, gather, 0)
+    lax.fori_loop(0, chunks, late_step, 0)
+
+    def pair_step(t, carry):
+        made = [gather(1 + 2 * t + i) for i in range(2)]
+        for i in range(2):
+            spread_out(1 + 2 * t + i, made[i])
+        return carry
+
+    lax.fori_loop(0, aggs // 2 - 1, pair_step, 0)
     for d in (2, 3):
 
         @pl.when(there[d])
         def _():
             mg_landing[d].wait_recv()
 
-    def finish(c, carry):
+    def finish(t, carry):
+        c = jnp.where(t == 0, 0, jnp.where(t == 1, chunks - 1, t - 1))
         for d in range(2):
 
             @pl.when(there[d])
             def _():
-                ms_copy(d, c, True).wait_recv()
+                for late in range(2):
+                    ms_copy(d, c, late, True).wait_recv()
 
         for i in range(2):
             g = 2 * c + i
-            b0, b1, b2 = (rmsg[0, c, 3 * i + n].astype(F32) for n in range(3))
-            f0, f1, f2 = (rmsg[1, c, 3 * i + n].astype(F32) for n in range(3))
-            b3, f3 = rmsg[0, c, 6].astype(F32), rmsg[1, c, 6].astype(F32)
+            be, bz, fe, fz = (rmsg[d, c, n].astype(F32) for d in range(2) for n in (i, 4 + 2 * i))
+            b0, f0 = (rmsg[d, c, 3 + 2 * i].astype(F32) for d in range(2))
+            b3, f3 = (rmsg[d, c, 2].astype(F32) for d in range(2))
             if i == 1:
                 b3, f3 = swap_halves(b3), swap_halves(f3)
+            b1, f1 = jnp.where(low, be, swap_halves(bz)), jnp.where(low, fe, swap_halves(fz))
+            b2, f2 = jnp.where(low, swap_halves(be), bz), jnp.where(low, swap_halves(fe), fz)
             l0, l1, l2, l3 = (gl[g, n].astype(F32) for n in range(4))
             r0, r1, r2, r3 = (gr[g + 1, n].astype(F32) for n in range(4))
             tiles = (
@@ -385,7 +470,8 @@
             if d < 2:
                 for c in range(chunks):
                     ps_copy(d, c).wait_send()
-                    ms_copy(d, c).wait_send()
+                    for late in range(2):
+                        ms_copy(d, c, late).wait_send()
             else:
                 pg_copy(d).wait_send()
                 mg_copies[d].wait_send()
@@ -412,6 +498,7 @@
             pltpu.VMEM((4, cols + 2, 16, 128), BF16),
             pltpu.VMEM((2, cols, B, 128), BF16),
             pltpu.VMEM((2, aggs, 128, 128), BF16),
+            pltpu.VMEM((2, cols, B, 384), F32),
             pltpu.VMEM((aggs, 5, 2, 128, 128), BF16),
             pltpu.VMEM((2, chunks, 7, B, 128), BF16),
             pltpu.VMEM((2, chunks, 7, B, 128), BF16),
@@ -425,8 +512,8 @@
             dma((2, chunks)),
             dma((2,)),
             dma((2,)),
-            dma((2, chunks)),
-            dma((2, chunks)),
+            dma((2, chunks, 2)),
+            dma((2, chunks, 2)),
             dma((2,)),
             dma((2,)),
         ],

time: 19 us -> 16.8 us (0.88)
  the two profiles are of different devices: /device:TPU:24 before, /device:TPU:1 now
where the time goes in v3:
time: 16.8 us; the launch traced here: 16.7 us
  Pallas kernels  15.5 us (92%)
  local copies, waits for them, and re-layouts  1.19 us (7%)
    pallas_call x1, Pallas kernels, local(): pl.pallas_call(functools.partial(kernel, n_sub, n_gy, cols), out_shape=ja...  15.5 us
    unnamed x1, local copies, waits for them, and re-layouts  1.19 us

profile of v3, /device:TPU:1, one launch (start us, length us, event | category | flops | bytes accessed | tf_op | source)
XLA Modules:
  0.0 16.7 jit_solution(7117526690268621855)
XLA Ops:
  0.0 15.5 %shard_map.37 = bf16[1,8,64,1600]{3,2,1,0:T(8,128)(2,1)S(1)} custom-call(bf16[2,16,64,320]{3,2,1,0:T(8,128)(2,1)} %a_hbm.1, bf16[2,16,64,128]{3,2,1,0:T(8,128)(2,1)} %p_hbm.1, s32[2,16]{1,0:T(2,128)} %sp_hbm.1), custom_call_target="tpu_custom_call" | custom-call | flops 1300000000 | bytes 4000000 | tf_op jit(solution)/shard_map/pallas_call | solution.py:487
  15.5 1.2 %copy.5 = bf16[1,8,64,1600]{3,2,1,0:T(8,128)(2,1)} copy(bf16[1,8,64,1600]{3,2,1,0:T(8,128)(2,1)S(1)} %shard_map.37) | data formatting | bytes 3276800

commit v4 on v3

--- a/solution.py
+++ b/solution.py
@@ -47,7 +47,7 @@
 def kernel(
     n_sub, n_gy, cols,
     a_hbm, p_hbm, sp_hbm, out,
-    a_v, pe, sp_own, sp_h, m0t, m1t, turn, flip, part, gs, msg, rmsg, acc, gl, gr,
+    a_v, pe, sp_own, sp_h, m0t, m1t, turn, flip, part, facing, msg, rmsg, acc, gl, gr,
     local_sem, sp_send, sp_recv, ps_send, ps_recv, pg_send, pg_recv,
     ms_send, ms_recv, mg_send, mg_recv,
 ):
@@ -78,11 +78,6 @@
     get_sp.start()
     get_p.start()
     get_a.start()
-    get_sp.wait()
-    get_p.wait()
-    ones = [jnp.where(t, 1, 0).astype(jnp.int32) for t in there]
-    pl.semaphore_wait(barrier, ones[0] + ones[1] + ones[2] + ones[3])
-
     def remote(src, dst, send, recv, device):
         return pltpu.make_async_remote_copy(
             src_ref=src, dst_ref=dst, send_sem=send, recv_sem=recv, device_id=device, device_id_type=MESH
@@ -122,38 +117,6 @@
         2: remote(gl.at[aggs], gl.at[0], mg_send.at[0], mg_recv.at[0], around[2]),
         3: remote(gr.at[0], gr.at[aggs], mg_send.at[1], mg_recv.at[1], around[3]),
     }
-
-    for behind in range(2):
-
-        @pl.when(jnp.logical_and(slow == behind, there[behind]))
-        def _():
-            ps_copy(behind, 0).start()
-
-    for d in range(4):
-
-        @pl.when(there[d])
-        def _():
-            sp_copy(d).start()
-
-    for behind in range(2):
-
-        @pl.when(jnp.logical_and(slow == behind, there[behind]))
-        def _():
-            for c in order[1:]:
-                ps_copy(behind, c).start()
-
-    for d in (2, 3):
-
-        @pl.when(there[d])
-        def _():
-            pg_copy(d).start()
-
-    for behind in range(2):
-
-        @pl.when(jnp.logical_and(slow == 1 - behind, there[behind]))
-        def _():
-            for c in order:
-                ps_copy(behind, c).start()
 
     tile0 = jnp.zeros((B, 128), BF16)
     for d in range(4):
@@ -190,8 +153,6 @@
         for t in (0, 2, 10):
             out[0, g, :, 128 * t : 128 * t + 128] = tile0
         out[0, g, :, 1536:] = jnp.zeros((B, B), BF16)
-        gs[g, 4, 0] = jnp.zeros((128, 128), BF16)
-        gs[g, 3, 1] = jnp.zeros((128, 128), BF16)
 
     def masks_of_row(row, e):
         spill = spread(row, cols)
@@ -201,9 +162,36 @@
         m1t[e, 1] = spill[0] * side[0]
         m1t[e, cols] = spill[cols - 1] * side[1]
 
+    get_sp.wait()
     own = sp_own[...].astype(F32)
     masks_of_row(own[0:1], 1)
     masks_of_row(own[1:2], 2)
+    get_p.wait()
+    ones = [jnp.where(t, 1, 0).astype(jnp.int32) for t in there]
+    pl.semaphore_wait(barrier, ones[0] + ones[1] + ones[2] + ones[3])
+
+    for d in range(4):
+
+        @pl.when(there[d])
+        def _():
+            sp_copy(d).start()
+            if d > 1:
+                pg_copy(d).start()
+
+    for behind in range(2):
+
+        @pl.when(jnp.logical_and(slow == behind, there[behind]))
+        def _():
+            for c in order:
+                ps_copy(behind, c).start()
+
+    for behind in range(2):
+
+        @pl.when(jnp.logical_and(slow == 1 - behind, there[behind]))
+        def _():
+            for c in order:
+                ps_copy(behind, c).start()
+
 
     def prepare(t, carry):
         for r in range(2):
@@ -228,72 +216,74 @@
             return first, tile * tall(m1 * lo + hi), tile0
         return first, tile * tall(hi), tile * tall(m1 * lo)
 
-    def keep(r, g):
-        m0 = [m0t[1 + r, 1 + 2 * g + odd] for odd in range(2)]
-        return flip[r, g, B:] * tall(m0[0] * lo + m0[1] * hi)
-
-    def first_rows(r, c):
-        values = []
-        for i in range(2):
-            g = 2 * c + i
-            own = [inner(r, 2 * g + odd, odd) for odd in range(2)]
-            for odd in range(2):
-                y = 2 * g + odd
-                first, second, third = inner(1 - r, y, odd)
-                x_in = beside([tile0, second, third, first])
-                at = y - 1 + 2 * odd
-                tile = pe[1 + r, 1 + at]
-                m0, m1 = m0t[1 + r, 1 + at], m1t[1 + r, 1 + at]
-                if odd == 0:
-                    y_out = beside([tile0, tile * tall(lo + m1 * hi), tile * tall(m0 * hi), tile0])
-                else:
-                    y_out = beside([tile * tall(m0 * hi), tile * tall(m1 * hi), tile * tall(lo), tile0])
-                y_in = beside([*own[1 - odd], tile0])
-                x_out = beside([tile0] * 4)
-                blocks = [beside([*own[odd], tile0])]
-                blocks += [x_out, x_in] if r == 0 else [x_in, x_out]
-                blocks += [y_out, y_in] if odd == 0 else [y_in, y_out]
-                left = a_v[r, y]
-                value = jnp.dot(left[:, :256], below(blocks[:4]), preferred_element_type=F32)
-                value += jnp.dot(left[:, 256:], blocks[4], preferred_element_type=F32)
-                values.append(value)
-        return values
-
-    def first_step(c):
-        values = [first_rows(r, c) for r in range(2)]
-        leave = {}
-        for r in range(2):
-            for i in range(2):
-                pair = below([v[:, 128:].astype(BF16) for v in values[r][2 * i : 2 * i + 2]])
-                leave[r, i] = jnp.dot(keep(r, 2 * c + i), pair, preferred_element_type=F32)
-        for r in range(2):
-            for i in range(2):
-                for odd in range(2):
-                    value = values[r][2 * i + odd]
-                    part[r, 4 * c + 2 * i + odd] = value[:, :384]
-                    gs[2 * c + i, 1 - r, r, B * odd : B * odd + B] = value[:, 384:].astype(BF16)
-                msg[r, c, i] = beside([leave[r, i][:, :B], leave[r, i][:, 128 : 128 + B]]).astype(BF16)
-            msg[r, c, 2] = beside([leave[r, i][:, 256 : 256 + B] for i in range(2)]).astype(BF16)
-        depart(c, 0)
-
-    def last_rows(r, c):
-        made = []
-        for i in range(2):
-            for odd in range(2):
-                y = 4 * c + 2 * i + odd
-                tile = pe[3 * r, 1 + y]
-                m0, m1 = m0t[3 * r, 1 + y], m1t[3 * r, 1 + y]
-                middle = tile * tall(m0 * hi)
-                if odd == 0:
-                    x_out = beside([tile * tall(lo), middle, tile * tall(m1 * hi)])
-                else:
-                    x_out = beside([tile * tall(lo + m1 * hi), middle, tile0])
-                none = beside([tile0] * 3)
-                left = a_v[r, y, :, :128] if r == 0 else a_v[r, y, :, 128:256]
-                right = below([none, x_out] if r == 0 else [x_out, none])
-                value = jnp.dot(left, right, preferred_element_type=F32)
-                made.append((part[r, y] + value).astype(BF16))
-        return made
+    def spills(r, g):
+        return [(m0t[1 + r, 1 + 2 * g + odd], m1t[1 + r, 1 + 2 * g + odd]) for odd in range(2)]
+
+    half0 = jnp.zeros((B, B), BF16)
+
+    def leaving(r, g):
+        (m0e, _), (m0o, _) = spills(r, g)
+        return flip[r, g, B:] * tall(m0e * lo + m0o * hi)
+
+    def staying(r, g):
+        (_, m1e), (_, m1o) = spills(r, g)
+        second = flip[r, g, B:]
+        return below([flip[r, g, :B], second * tall(m1e * lo), second * tall(m1o * hi)])
+
+    def operator(r, g):
+        even, odd = a_v[r, 2 * g], a_v[r, 2 * g + 1]
+        return below([
+            beside([even, half0, tile0]),
+            beside([odd[:, 192:256], half0, tile0, odd[:, :128], odd[:, 128:192], odd[:, 256:]]),
+        ])
+
+    def outside(r, g):
+        blocks = []
+        for odd in range(2):
+            y = 2 * g + odd
+            tile = pe[3 * r, 1 + y]
+            m0, m1 = m0t[3 * r, 1 + y], m1t[3 * r, 1 + y]
+            middle = tile * tall(m0 * hi)
+            if odd == 0:
+                blocks.append(beside([tile * tall(lo), middle, tile * tall(m1 * hi)]))
+            else:
+                blocks.append(beside([tile * tall(lo + m1 * hi), middle, tile0]))
+        return blocks
+
+    def columns(r, g, halo):
+        into = []
+        for odd in range(2):
+            first, second, third = inner(1 - r, 2 * g + odd, odd)
+            into.append(beside([tile0, second, third, first]))
+        out = [beside([b, tile0]) for b in outside(r, g)] if halo else [beside([tile0] * 4)] * 2
+        minus, plus = (out, into) if r == 0 else (into, out)
+        own = [beside([*inner(r, 2 * g + odd, odd), tile0]) for odd in range(2)]
+        tile = pe[1 + r, 2 * g]
+        m0, m1 = m0t[1 + r, 2 * g], m1t[1 + r, 2 * g]
+        prior = beside([tile0, tile * tall(lo + m1 * hi), tile * tall(m0 * hi), tile0])
+        tile = pe[1 + r, 2 * g + 3]
+        m0, m1 = m0t[1 + r, 2 * g + 3], m1t[1 + r, 2 * g + 3]
+        following = beside([tile * tall(m0 * hi), tile * tall(m1 * hi), tile * tall(lo), tile0])
+        return below([own[0], minus[0], plus[0], prior, own[1], minus[1], plus[1], following])
+
+    units = [(r, i) for i in range(2) for r in range(2)]
+
+    def first_step(some):
+        value, leave = {}, {}
+        every = [(r, 2 * c + i) for c in some for r, i in units]
+        for r, g in every:
+            value[r, g] = jnp.dot(leaving(r, g), operator(r, g), preferred_element_type=F32).astype(BF16)
+        for r, g in every:
+            leave[r, g] = jnp.dot(value[r, g], columns(r, g, False), preferred_element_type=F32)
+        for r, g in every:
+            kept, sent = value[r, g], leave[r, g]
+            facing[r, g] = beside([kept[:, 128 * n : 128 * n + 128] for n in (r, 2 + r)])
+            part[r, g] = sent[:, :384]
+            msg[r, g // 2, g % 2] = beside([sent[:, 128 : 128 + B], sent[:, 256 : 256 + B]]).astype(BF16)
+        for c in some:
+            for r in range(2):
+                msg[r, c, 2] = beside([leave[r, 2 * c + i][:, 384 : 384 + B] for i in range(2)]).astype(BF16)
+            depart(c, 0)
 
     def last_step(c):
         for r in range(2):
@@ -302,21 +292,27 @@
             def _():
                 ps_copy(r, c, True).wait_recv()
 
-        made = [last_rows(r, c) for r in range(2)]
         leave = {}
-        for r in range(2):
-            for i in range(2):
-                leave[r, i] = jnp.dot(
-                    keep(r, 2 * c + i), below(made[r][2 * i : 2 * i + 2]), preferred_element_type=F32
-                )
-        for r in range(2):
-            for i in range(2):
-                for n, place in enumerate((r, 2, 3 + r)):
-                    for odd in range(2):
-                        gs[2 * c + i, place, r, B * odd : B * odd + B] = made[r][2 * i + odd][:, 128 * n : 128 * n + 128]
-                msg[r, c, 3 + 2 * i] = leave[r, i][:, :128].astype(BF16)
-                msg[r, c, 4 + 2 * i] = beside([leave[r, i][:, 128 + B : 256], leave[r, i][:, 256 + B :]]).astype(BF16)
+        none = beside([tile0] * 3)
+        for r, i in units:
+            even, odd = outside(r, 2 * c + i)
+            right = below([none, even, none, odd] if r == 0 else [even, none, odd, none])
+            leave[r, i] = jnp.dot(facing[r, 2 * c + i], right, preferred_element_type=F32)
+        for r, i in units:
+            sent = part[r, 2 * c + i] + leave[r, i]
+            msg[r, c, 3 + 2 * i] = sent[:, :128].astype(BF16)
+            msg[r, c, 4 + 2 * i] = beside([sent[:, 128 + B : 256], sent[:, 256 + B :]]).astype(BF16)
         depart(c, 1)
+
+    def own_step(some):
+        value, made = {}, {}
+        every = [(r, g) for g in some for r in range(2)]
+        for r, g in every:
+            value[r, g] = jnp.dot(staying(r, g), operator(r, g), preferred_element_type=F32).astype(BF16)
+        for r, g in every:
+            made[r, g] = jnp.dot(value[r, g], columns(r, g, True), preferred_element_type=F32)
+        for g in some:
+            spread_out(g, made[0, g], made[1, g])
 
     def depart(c, late):
         @pl.when(jnp.logical_and(slow == 1, there[1]))
@@ -331,20 +327,16 @@
         def _():
             ms_copy(1, c, late).start()
 
-    def middle_step(c, carry):
-        first_step(c)
-        return carry
-
-    lax.fori_loop(1, chunks - 1, middle_step, 0)
-
-    for d in range(4):
+    ends, middle = [0, chunks - 1], list(range(1, chunks - 1))
+    if middle:
+        first_step(middle)
+
+    for d in (2, 3):
 
         @pl.when(there[d])
         def _():
             sp_copy(d, True).wait_recv()
 
-    masks_of_row(sp_h[0, 1:2].astype(F32), 0)
-    masks_of_row(sp_h[1, 0:1].astype(F32), 3)
     for d, at, column in ((2, 0, cols - 1), (3, cols + 1, 0)):
         for r in range(2):
             spill = jnp.broadcast_to(sp_h[d, r : r + 1, column : column + 1].astype(F32), (16, 128)).astype(BF16)
@@ -357,76 +349,69 @@
         def _():
             pg_copy(d, True).wait_recv()
 
-    def end_step(t, carry):
-        first_step(t * (chunks - 1))
-        return carry
-
-    lax.fori_loop(0, 2, end_step, 0)
-
-
-    def gather(g):
-        right = beside([gs[g, n].reshape(256, 128) for n in range(5)])
-        m1 = [[m1t[1 + r, 1 + 2 * g + odd] for odd in range(2)] for r in range(2)]
-        left = below([
-            beside([flip[r, g, :B] for r in range(2)]),
-            beside([flip[r, g, B:] * tall(m1[r][0] * lo) for r in range(2)]),
-            beside([flip[r, g, B:] * tall(m1[r][1] * hi) for r in range(2)]),
-        ])
-        return jnp.dot(left, right, preferred_element_type=F32)
-
-    def spread_out(g, made):
-        def piece(rows, n):
-            return made[B * rows : B * rows + B, 128 * n : 128 * n + 128]
-
-        um, up, ce, d0, d1 = (swap_halves(piece(0, n)) for n in range(5))
+    first_step(ends)
+    for d in (0, 1):
+
+        @pl.when(there[d])
+        def _():
+            sp_copy(d, True).wait_recv()
+
+    masks_of_row(sp_h[0, 1:2].astype(F32), 0)
+    masks_of_row(sp_h[1, 0:1].astype(F32), 3)
+
+
+    def spread_out(g, before, after):
+        def tiles(rows):
+            b, a = (
+                [x[B * rows : B * rows + B, 128 * n : 128 * n + 128] for n in range(4)] for x in (before, after)
+            )
+            return b[0] + a[3], a[0] + b[3], b[1] + a[1], b[2], a[2]
+
+        um, up, ce, d0, d1 = (swap_halves(x) for x in tiles(0))
         acc[g, 0] = jnp.where(low, d0, um)
         acc[g, 1] = jnp.where(low, um, 0.0)
         acc[g, 2] = jnp.where(low, 0.0, ce)
         acc[g, 3] = jnp.where(low, ce, d0 + d1)
         acc[g, 4] = jnp.where(low, d1, up)
         acc[g, 5] = jnp.where(low, up, 0.0)
-        um, up, ce, d0, d1 = (piece(1, n) for n in range(5))
+        um, up, ce, d0, d1 = tiles(1)
         gr[g, 0] = jnp.where(low, um, d0).astype(BF16)
         gr[g, 1] = jnp.where(low, up, d1).astype(BF16)
         gr[g, 2] = ce.astype(BF16)
         gr[g, 3] = jnp.where(low, d0 + d1, 0.0).astype(BF16)
-        um, up, ce, d0, d1 = (piece(2, n) for n in range(5))
+        um, up, ce, d0, d1 = tiles(2)
         gl[g + 1, 0] = um.astype(BF16)
         gl[g + 1, 1] = up.astype(BF16)
         gl[g + 1, 2] = ce.astype(BF16)
         gl[g + 1, 3] = (d0 + d1).astype(BF16)
 
+    def nth(t):
+        return jnp.where(t == 0, 0, jnp.where(t == 1, chunks - 1, t - 1))
+
     def late_step(t, carry):
-        last_step(jnp.where(t == 0, 0, jnp.where(t == 1, chunks - 1, t - 1)))
-        for d, at in ((2, 0), (3, aggs - 1)):
-
-            @pl.when(t == d - 2)
-            def _():
-                spread_out(at, gather(at))
-
-                @pl.when(there[d])
-                def _():
-                    mg_copies[d].start()
-
+        last_step(nth(t))
         return carry
 
-    lax.fori_loop(0, chunks, late_step, 0)
-
-    def pair_step(t, carry):
-        made = [gather(1 + 2 * t + i) for i in range(2)]
-        for i in range(2):
-            spread_out(1 + 2 * t + i, made[i])
-        return carry
-
-    lax.fori_loop(0, aggs // 2 - 1, pair_step, 0)
+    lax.fori_loop(0, 2, late_step, 0)
+    own_step([0, aggs - 1])
     for d in (2, 3):
 
         @pl.when(there[d])
         def _():
+            mg_copies[d].start()
+
+    lax.fori_loop(2, chunks, late_step, 0)
+    inner_aggs = list(range(1, aggs - 1))
+    for first in range(0, aggs - 2, 3):
+        own_step(inner_aggs[first : first + 3])
+    for d in (2, 3):
+
+        @pl.when(there[d])
+        def _():
             mg_landing[d].wait_recv()
 
     def finish(t, carry):
-        c = jnp.where(t == 0, 0, jnp.where(t == 1, chunks - 1, t - 1))
+        c = nth(t)
         for d in range(2):
 
             @pl.when(there[d])
@@ -498,8 +483,8 @@
             pltpu.VMEM((4, cols + 2, 16, 128), BF16),
             pltpu.VMEM((2, cols, B, 128), BF16),
             pltpu.VMEM((2, aggs, 128, 128), BF16),
-            pltpu.VMEM((2, cols, B, 384), F32),
-            pltpu.VMEM((aggs, 5, 2, 128, 128), BF16),
+            pltpu.VMEM((2, aggs, B, 384), F32),
+            pltpu.VMEM((2, aggs, B, 256), BF16),
             pltpu.VMEM((2, chunks, 7, B, 128), BF16),
             pltpu.VMEM((2, chunks, 7, B, 128), BF16),
             pltpu.VMEM((aggs, 6, B, 128), F32),

time: 16.8 us -> 16.7 us (level)
  Pallas kernels: 15.5 us -> 15.3 us
where the time goes in v4:
time: 16.7 us; the launch traced here: 16.5 us
  Pallas kernels  15.3 us (92%)
  local copies, waits for them, and re-layouts  1.19 us (7%)
    pallas_call x1, Pallas kernels, local(): pl.pallas_call(functools.partial(kernel, n_sub, n_gy, cols), out_shape=ja...  15.3 us
    unnamed x1, local copies, waits for them, and re-layouts  1.19 us

profile of v4, /device:TPU:1, one launch (start us, length us, event | category | flops | bytes accessed | tf_op | source)
XLA Modules:
  0.0 16.5 jit_solution(14044771082526188185)
XLA Ops:
  0.0 15.3 %shard_map.37 = bf16[1,8,64,1600]{3,2,1,0:T(8,128)(2,1)S(1)} custom-call(bf16[2,16,64,320]{3,2,1,0:T(8,128)(2,1)} %a_hbm.1, bf16[2,16,64,128]{3,2,1,0:T(8,128)(2,1)} %p_hbm.1, s32[2,16]{1,0:T(2,128)} %sp_hbm.1), custom_call_target="tpu_custom_call" | custom-call | flops 1300000000 | bytes 4000000 | tf_op jit(solution)/shard_map/pallas_call | solution.py:472
  15.4 1.2 %copy.5 = bf16[1,8,64,1600]{3,2,1,0:T(8,128)(2,1)} copy(bf16[1,8,64,1600]{3,2,1,0:T(8,128)(2,1)S(1)} %shard_map.37) | data formatting | bytes 3276800

commit v5 on v4

--- a/solution.py
+++ b/solution.py
@@ -170,7 +170,13 @@
     ones = [jnp.where(t, 1, 0).astype(jnp.int32) for t in there]
     pl.semaphore_wait(barrier, ones[0] + ones[1] + ones[2] + ones[3])
 
-    for d in range(4):
+    for behind in range(2):
+
+        @pl.when(jnp.logical_and(slow == behind, there[behind]))
+        def _():
+            ps_copy(behind, 0).start()
+
+    for d in (2, 3, 0, 1):
 
         @pl.when(there[d])
         def _():
@@ -182,7 +188,7 @@
 
         @pl.when(jnp.logical_and(slow == behind, there[behind]))
         def _():
-            for c in order:
+            for c in order[1:]:
                 ps_copy(behind, c).start()
 
     for behind in range(2):
@@ -410,8 +416,7 @@
         def _():
             mg_landing[d].wait_recv()
 
-    def finish(t, carry):
-        c = nth(t)
+    def finish(c):
         for d in range(2):
 
             @pl.when(there[d])
@@ -443,9 +448,9 @@
             )
             for t, value in tiles:
                 out[0, g, :, 128 * t : 128 * t + 128] = value.astype(BF16)
-        return carry
-
-    lax.fori_loop(0, chunks, finish, 0)
+
+    for c in order:
+        finish(c)
 
     for d in range(4):
 

time: 16.7 us -> 16.7 us (level)
  no operation moved by 1% of the time
where the time goes in v5:
time: 16.7 us; the launch traced here: 16.6 us
  Pallas kernels  15.4 us (92%)
  local copies, waits for them, and re-layouts  1.19 us (7%)
    pallas_call x1, Pallas kernels, local(): pl.pallas_call(functools.partial(kernel, n_sub, n_gy, cols), out_shape=ja...  15.4 us
    unnamed x1, local copies, waits for them, and re-layouts  1.19 us

profile of v5, /device:TPU:1, one launch (start us, length us, event | category | flops | bytes accessed | tf_op | source)
XLA Modules:
  0.0 16.6 jit_solution(4864633703162656165)
XLA Ops:
  0.0 15.4 %shard_map.37 = bf16[1,8,64,1600]{3,2,1,0:T(8,128)(2,1)S(1)} custom-call(bf16[2,16,64,320]{3,2,1,0:T(8,128)(2,1)} %a_hbm.1, bf16[2,16,64,128]{3,2,1,0:T(8,128)(2,1)} %p_hbm.1, s32[2,16]{1,0:T(2,128)} %sp_hbm.1), custom_call_target="tpu_custom_call" | custom-call | flops 1300000000 | bytes 4000000 | tf_op jit(solution)/shard_map/pallas_call | solution.py:477
  15.4 1.2 %copy.5 = bf16[1,8,64,1600]{3,2,1,0:T(8,128)(2,1)} copy(bf16[1,8,64,1600]{3,2,1,0:T(8,128)(2,1)S(1)} %shard_map.37) | data formatting | bytes 3276800
